TPU v7x, 32 devices: a whole 2x2x4 slice. The times are simulated.
32 devices in a mesh: expert: 4 (over y, x), shard: 8 (over z, core).
Axes of the slice: x: 2, y: 2, z: 4, core: 2. Of those that a mesh axis runs over, the one named last changes fastest.
Arguments:
- grad_out: bfloat16 [4, 1024, 3072], P('expert', 'shard'), may hold values from -6 to 6
- gate_pre: bfloat16 [4, 1024, 8192], P('expert', None, 'shard'), may hold values from -8 to 8
- up_pre: bfloat16 [4, 1024, 8192], P('expert', None, 'shard'), may hold values from -6 to 6
- counts: int32 [4, 8], P('expert', 'shard'), may hold values from 32 to 128
- placement: int32 [4], replicated, may hold values from 0 to 63, as said below
- master: float32 [4, 8192, 3072], P('expert', 'shard')
Outputs:
- d_gate: bfloat16 [4, 1024, 8192], P('expert', None, 'shard')
- d_up: bfloat16 [4, 1024, 8192], P('expert', None, 'shard')
- new_master: float32 [4, 8192, 3072], P('expert', 'shard')
Inputs may be any that keep to these rules, and one draw needn't show every extreme that they name: `placement`: slots that hold the same expert form aligned blocks of 1, 2 or 4 consecutive slots, each block starting at a multiple of its size; different blocks hold different experts.
All inputs are finite; a program needn't handle non-finite values.
Results may differ from a plain program's by a relative error of at most 0.006.
Values may be sent and summed in bfloat16 or wider, within the bound.
No kernel may reach another device: no remote copies, remote signals or barrier semaphores. Data moves between devices by JAX's collectives and lax.ppermute only.
A program may use at most 256 MiB of HBM per device.

v0:
```python
import functools

import jax
import jax.numpy as jnp
from jax import lax
from jax.experimental import pallas as pl
from jax.experimental.pallas import tpu as pltpu
from jax.sharding import PartitionSpec as P

learn_rate = 0.02
rms_eps = 1e-06
tall = 256
params = pltpu.CompilerParams(vmem_limit_bytes=56 * 2**20)


def dot(a, b, dims):
    return lax.dot_general(a, b, (dims, ((), ())), preferred_element_type=jnp.float32)


def hidden_kernel(gate_ref, up_ref, out_ref):
    gate = gate_ref[0].astype(jnp.float32)
    hidden = gate * jax.nn.sigmoid(gate) * up_ref[0].astype(jnp.float32)
    out_ref[...] = hidden.T.astype(out_ref.dtype)


def hidden_transposed(gate_pre, up_pre):
    _, rows, ffw = gate_pre.shape
    block = pl.BlockSpec((1, tall, ffw), lambda i: (0, i, 0))
    return pl.pallas_call(
        hidden_kernel,
        grid=(rows // tall,),
        in_specs=[block, block],
        out_specs=pl.BlockSpec((ffw, tall), lambda i: (0, i)),
        out_shape=jax.ShapeDtypeStruct((ffw, rows), jnp.bfloat16),
        compiler_params=params,
    )(gate_pre, up_pre)


def update_rows(master, grads, out_ref):
    square = sum(jnp.sum(g * g, axis=1, keepdims=True) for g in grads)
    scale = learn_rate / jnp.sqrt(square / master.shape[1] + rms_eps)
    first = 0
    for grad in grads:
        cols = slice(first, first + grad.shape[1])
        out_ref[0, :, cols] = master[:, cols] - grad * scale
        first += grad.shape[1]


def gates_back(d_hidden, gate_ref, up_ref, gate_out, up_out):
    gate = gate_ref[0].astype(jnp.float32)
    up = up_ref[0].astype(jnp.float32)
    sig = jax.nn.sigmoid(gate)
    up_out[0] = (d_hidden * (gate * sig)).astype(up_out.dtype)
    slope = sig * (1.0 + gate * (1.0 - sig))
    gate_out[0] = (d_hidden * up * slope).astype(gate_out.dtype)


def phase_kernel(n_pieces, layout, wide, blocks, tall, grad_in, ready, gates, update, flag_ref,
                 *refs):
    refs = list(refs)
    pieces = [refs.pop(0) for _ in range(n_pieces)]
    hidden_ref = refs.pop(0) if blocks else None
    master_hbm = refs.pop(0) if gates or update else None
    grad_ref = refs.pop(0) if grad_in else None
    ready_ref = refs.pop(0) if ready else None
    gate_ref, up_ref = (refs.pop(0), refs.pop(0)) if gates else (None, None)
    gate_out, up_out = (refs.pop(0), refs.pop(0)) if gates else (None, None)
    out_ref = refs.pop(0) if blocks else None
    whole_ref, sem_ref = refs[:2]
    master_ref, master_sem = refs[2:4] if gates or update else (None, None)
    sum_ref = refs[4] if update else None
    step = pl.program_id(0)
    by_block = {}
    for place, (ref, index, row, source_first, first, count) in enumerate(layout):
        source = pieces[ref] if index is None else pieces[ref].at[index]
        high = source.shape[0]
        start = row if isinstance(row, int) else pl.multiple_of(flag_ref[row[0]], 128)
        copy = pltpu.make_async_copy(
            source.at[:, pl.ds(source_first, count)],
            whole_ref.at[pl.ds(start, high), pl.ds(first, count)],
            sem_ref.at[place],
        )
        by_block.setdefault(first // wide, []).append(copy)
    master_copies = []
    if gates or update:
        for i in range(master_ref.shape[0] // tall):
            lines = pl.ds(i * tall, tall)
            master_copies.append(
                pltpu.make_async_copy(
                    master_hbm.at[0, lines], master_ref.at[lines], master_sem.at[i]
                )
            )

    @pl.when(step == 0)
    def _():
        for block in sorted(by_block):
            for copy in by_block[block]:
                copy.start()
        for copy in master_copies:
            copy.start()

    for block in sorted(by_block):

        @pl.when(step == min(block, blocks))
        def _(block=block):
            for copy in by_block[block]:
                copy.wait()

    for i, copy in enumerate(master_copies):

        @pl.when(step == blocks + i)
        def _(copy=copy):
            copy.wait()

    if ready:

        @pl.when(step == 0)
        def _():
            sum_ref[:, :wide] = ready_ref[...].astype(jnp.float32)

    if blocks:

        @pl.when((step >= ready) & (step < blocks))
        def _():
            cols = pl.ds(pl.multiple_of(step * wide, wide), wide)
            grad = dot(hidden_ref[...], whole_ref[:, cols], ((1,), (0,)))
            if grad_in:
                own = grad_ref[...].astype(jnp.float32)
                grad = own + jnp.where(flag_ref[0] > 0, grad, 0.0)
            if update:
                sum_ref[:, cols] = grad
            else:
                out_ref[...] = grad.astype(out_ref.dtype)

    if gates or update:

        @pl.when(step >= blocks)
        def _():
            lines = pl.ds(pl.multiple_of((step - blocks) * tall, tall), tall)
            if update:
                update_rows(master_ref[lines, :], [sum_ref[lines, :]], out_ref)
            if gates:
                weight = master_ref[lines, :].astype(jnp.bfloat16)
                d_hidden = dot(whole_ref[...], weight, ((1,), (1,)))
                gates_back(d_hidden, gate_ref, up_ref, gate_out, up_out)


def phase_call(flags, pieces, layout, hidden=None, master=None, grad=None, gate_up=None,
               ready=None, update=False, d_model=None, tall=256):
    if master is not None:
        _, ffw, d_model = master.shape
    else:
        ffw = hidden.shape[0]
    rows = gate_up[0].shape[1] if hidden is None else hidden.shape[1]
    wide = next(w for w in (1024, 768, 512, 128) if d_model % w == 0)
    blocks = d_model // wide if hidden is not None else 0
    lines = ffw // tall if master is not None else 0
    cut = []
    for ref, index, row, first, count in layout:
        piece = wide if blocks else count
        for at in range(0, count, piece):
            cut.append((ref, index, row, at, first + at, piece))
    row_block = lambda i: jnp.maximum(i - blocks, 0)
    col_block = lambda i: jnp.minimum(i, blocks - 1)
    anywhere = pl.BlockSpec(memory_space=pl.ANY)
    side = pl.BlockSpec((1, rows, tall), lambda i, flag: (0, 0, row_block(i)))
    full = pl.BlockSpec((1, tall, d_model), lambda i, flag: (0, row_block(i), 0))
    column = pl.BlockSpec((ffw, wide), lambda i, flag: (0, col_block(i)))
    specs, args = [anywhere] * len(pieces), list(pieces)
    out_specs, out_shape = [], []
    scratch = [
        pltpu.VMEM((rows, d_model), jnp.bfloat16),
        pltpu.SemaphoreType.DMA((len(cut),)),
    ]
    if hidden is not None:
        specs.append(pl.BlockSpec((ffw, rows), lambda i, flag: (0, 0), pipeline_mode=pl.Buffered(1)))
        args.append(hidden)
    if master is not None:
        specs.append(anywhere)
        args.append(master)
        scratch.append(pltpu.VMEM((ffw, d_model), jnp.float32))
        scratch.append(pltpu.SemaphoreType.DMA((lines,)))
    if grad is not None:
        specs.append(column)
        args.append(grad)
    if ready is not None:
        specs.append(pl.BlockSpec((ffw, wide), lambda i, flag: (0, 0)))
        args.append(ready)
    if gate_up is not None:
        specs += [side, side]
        args += list(gate_up)
        out_specs += [side, side]
        out_shape += [jax.ShapeDtypeStruct(a.shape, a.dtype) for a in gate_up]
    if update:
        out_specs.append(full)
        out_shape.append(jax.ShapeDtypeStruct(master.shape, master.dtype))
        scratch.append(pltpu.VMEM((ffw, d_model), jnp.float32))
    elif hidden is not None:
        out_specs.append(column)
        out_shape.append(jax.ShapeDtypeStruct((ffw, d_model), jnp.bfloat16))
    dots = (hidden is not None) + (gate_up is not None)
    return pl.pallas_call(
        functools.partial(
            phase_kernel, len(pieces), cut, wide, blocks, tall, grad is not None,
            0 if ready is None else 1, gate_up is not None, update,
        ),
        grid_spec=pltpu.PrefetchScalarGridSpec(
            num_scalar_prefetch=1,
            grid=(blocks + lines,),
            in_specs=specs,
            out_specs=out_specs,
            scratch_shapes=scratch,
        ),
        out_shape=out_shape,
        compiler_params=params,
        cost_estimate=pl.CostEstimate(
            flops=2 * dots * rows * ffw * d_model,
            bytes_accessed=8 * ffw * d_model,
            transcendentals=0,
        ),
    )(flags, *args)


def update_kernel(master_ref, *refs):
    update_rows(master_ref[0], [r[...].astype(jnp.float32) for r in refs[:-1]], refs[-1])


def update_call(master, grads):
    _, ffw, d_model = master.shape
    full = pl.BlockSpec((1, 128, d_model), lambda i: (0, i, 0))
    part = pl.BlockSpec((128, grads[0].shape[1]), lambda i: (i, 0))
    return pl.pallas_call(
        update_kernel,
        grid=(ffw // 128,),
        in_specs=[full] + [part] * len(grads),
        out_specs=full,
        out_shape=jax.ShapeDtypeStruct(master.shape, master.dtype),
        compiler_params=params,
    )(master, *grads)


def after(value, other):
    return lax.optimization_barrier((value, other))[0]


def per_device(grad_out, gate_pre, up_pre, counts, placement, master):
    n_slot = lax.axis_size("expert")
    n_shard = lax.axis_size("shard")
    chips = n_shard // 2
    core = lax.axis_index("shard") % 2
    chip = lax.axis_index("shard") // 2
    slot = lax.axis_index("expert")
    rows, d_model = grad_out.shape[1:]
    order = jnp.arange(n_slot, dtype=jnp.int32)
    same = placement[:, None] == placement[None, :]
    pair_count = jnp.sum(same & (order[:, None] ^ 1 == order[None, :]), dtype=jnp.int32)
    four_count = jnp.sum(same & (order[:, None] ^ 2 == order[None, :]), dtype=jnp.int32)

    def share(bit):
        return jnp.any(same & (order[:, None] == slot) & (order[None, :] == slot ^ bit))

    orders = {}

    def send(value, axis, pairs):
        turn = orders.get((axis, *sorted(pairs)), 0)
        orders[(axis, *sorted(pairs))] = turn + 1
        turn, back = divmod(turn, 2)
        pairs = pairs[turn:] + pairs[:turn]
        return lax.ppermute(value, axis, pairs[::-1] if back else pairs)

    def to_slot(value, bit):
        return send(value, "expert", [(i, i ^ bit) for i in range(n_slot)])

    def to_core(value):
        return send(value, "shard", [(i, i ^ 1) for i in range(n_shard)])

    def to_chip(value, pairs):
        return send(value, "shard", [(2 * a + c, 2 * b + c) for a, b in pairs for c in range(2)])

    def along_chips(block, held=None):
        if chips != 4:
            return [block] + [
                to_chip(block, [((z + far) % chips, z) for z in range(chips)])
                for far in range(1, chips)
            ]
        two = to_chip(block, [(0, 2), (1, 3), (2, 0), (3, 1)])
        one = to_chip(block, [(1, 0), (2, 1), (3, 2)])
        three = to_chip(block, [(0, 1), (1, 2), (2, 3)])
        end = to_chip(two if held is None else after(two, held), [(2, 3), (1, 0)])
        one = jnp.where(chip == 3, end, one)
        three = jnp.where(chip == 0, end, three)
        return [block, one, two, three]

    def all_sum(grad):
        half = grad.shape[0] // 2
        done = []
        for part, bits in ((grad[:half], (1, 2)), (grad[half:], (2, 1))):
            sides = [jnp.where(slot & bit > 0, 1, 0) for bit in bits]
            for bit, side in zip(bits, sides):
                high = part.shape[0] // 2
                keep = lax.dynamic_slice_in_dim(part, side * high, high)
                send = lax.dynamic_slice_in_dim(part, (1 - side) * high, high)
                got = to_slot(send, bit)
                part = (keep.astype(jnp.float32) + got.astype(jnp.float32)).astype(part.dtype)
            for bit, side in zip(bits[::-1], sides[::-1]):
                got = to_slot(part, bit)
                part = jnp.concatenate(
                    [jnp.where(side == 0, part, got), jnp.where(side == 0, got, part)]
                )
            done.append(part)
        return jnp.concatenate(done)

    def body(mode, grad_out, gate_pre, up_pre, counts, placement, master):
        orders.clear()
        live = jnp.arange(rows, dtype=jnp.int32) < counts[0, 0]
        masked = jnp.where(live[:, None], grad_out[0], jnp.zeros((), grad_out.dtype))

        def gather(block):
            return lax.all_gather(block, "shard", axis=0, tiled=True)

        gate_up = (gate_pre, up_pre)
        if mode == "pair":
            width = d_model // 3
            early = to_slot(masked[:, 2 * width :], 1)
            hidden = hidden_transposed(gate_pre, up_pre)
            theirs = to_slot(after(hidden, early), 1)
            one = gather(masked[:, :width])
            two = gather(after(masked[:, width:], one))
            last = gather(after(early, two))
            half = one.shape[0] // 2

            def to_partner(whole):
                return to_slot(lax.dynamic_slice(whole, (core * half, 0), (half, width)), 1)

            first = to_partner(one)
            second = to_partner(two)
            flags = jnp.stack([share(1).astype(jnp.int32), core * half, (1 - core) * half])
            layout = [(0, None, 0, 0, width), (1, None, 0, width, 2 * width)]
            d_gate, d_up, grad = phase_call(
                flags, after([one, two], theirs), layout, hidden, master, gate_up=gate_up,
                tall=512,
            )
            layout = [(0, None, (1,), 0, width), (1, None, (2,), 0, width)]
            ready = phase_call(
                flags, [first, to_core(first)], layout, theirs, grad=grad, d_model=width
            )[0]
            second = after(second, grad)
            layout = [
                (0, None, (1,), width, width),
                (1, None, (2,), width, width),
                (2, None, 0, 2 * width, width),
            ]
            fresh = phase_call(
                flags, [second, to_core(second), last], layout, theirs, master, grad=grad,
                ready=ready, update=True,
            )[0]
            return d_gate, d_up, fresh
        hidden = hidden_transposed(gate_pre, up_pre)
        flags = jnp.zeros((1,), jnp.int32)
        if mode == "none":
            layout = [(0, None, 0, 0, d_model)]
            return tuple(
                phase_call(
                    flags, [gather(masked)], layout, hidden, master, gate_up=gate_up, update=True
                )
            )
        half = d_model // 2
        one = gather(masked[:, :half])
        two = gather(after(masked[:, half:], one))
        layout = [(0, None, 0, 0, half)]
        grads = []
        for whole in (one, two):
            grad = phase_call(flags, [whole], layout, hidden, d_model=half)[0]
            if mode == "four":
                grad = all_sum(grad)
            else:
                for bit in (1, 2):
                    got = to_slot(grad, bit)
                    grad = grad + jnp.where(share(bit), got, jnp.zeros((), got.dtype))
            grads.append(grad)
        layout = layout + [(1, None, 0, half, half)]
        d_gate, d_up = phase_call(flags, [one, two], layout, master=master, gate_up=gate_up, tall=512)
        return d_gate, d_up, update_call(master, grads)

    modes = ["none", "pair", "four"] + (["mixed"] if n_slot > 4 else [])
    mixed = jnp.where(four_count == n_slot, 2, len(modes) - 1)
    which = jnp.where(four_count > 0, mixed, jnp.where(pair_count > 0, 1, 0))
    return lax.switch(
        which,
        [lambda *a, mode=mode: body(mode, *a) for mode in modes],
        grad_out, gate_pre, up_pre, counts, placement, master,
    )


def solution(mesh):
    return jax.shard_map(
        per_device,
        mesh=mesh,
        in_specs=(
            P("expert", "shard", None),
            P("expert", None, "shard"),
            P("expert", None, "shard"),
            P("expert", "shard"),
            P(),
            P("expert", "shard", None),
        ),
        out_specs=(
            P("expert", None, "shard"),
            P("expert", None, "shard"),
            P("expert", "shard", None),
        ),
        check_vma=False,
    )
```

profile of v0, /device:TPU:0, one launch (start us, length us, event | category | flops | bytes accessed | tf_op | source)
XLA Modules:
  0.0 186.7 jit_solution(18145116909230247704)
XLA Ops:
  7.2 0.8 broadcast_compare_fusion.2
  8.0 1.4 convert_reduce_fusion
  10.7 169.4 %conditional.1 = ((bf16[1,1024,1024]{2,1,0:T(8,128)(2,1)}, bf16[1,1024,1024]{2,1,0:T(8,128)(2,1)}, f32[1,1024,3072]{2,1,0:T(8,128)})) conditional(s32[]{:T(128)} %clamp.3, (s32[1,1]{1,0:T(1,128)}, bf16[1,128,3072]{2,1,0:T(8,128)(2,1)}, bf16[1,1024,1024]{2,1,0:T(8,128)(2,1)}, bf16[1,1024,1024]{2,1,0:T(8,128)(2,1)}, ...), branch_computations={%region_2.3_spmd, %region_3.5_spmd, %region_5.6_spmd} | conditional | flops 21475229696 | bytes 226756256 | solution.py:388
  10.8 0.0 all-gather.9.cloned.1.call-start
  10.8 0.7 iota_compare_fusion.1
  11.5 0.0 copy-start.1
  11.5 1.4 bitcast_select_fusion.1
  12.9 0.7 fusion.2
  13.6 0.0 all-gather.9.cloned.1.call-update
  13.6 0.0 all-gather.11.cloned.1.call-start
  13.7 0.8 slice.28
  14.5 31.1 %all-gather.9.cloned.1.call-done.refs_0_ = bf16[1024,1024]{1,0:T(8,128)(2,1)} async-done(((bf16[128,1024]{1,0:T(8,128)(2,1)}), bf16[1024,1024]{1,0:T(8,128)(2,1)}) %all-gather.9.cloned.1.call-update) | async-done | bytes 2097168 | tf_op jit(solution)/shard_map/cond/branch_1_fun/all_gather | solution.py:319
  45.6 0.0 all-gather.11.cloned.1.call-update
  45.6 0.2 all-gather.13.cloned.1.call-start
  45.9 1.5 collective-permute-start
  47.4 0.0 copy-done.1
  47.4 4.3 %branch_1_fun.4.refs_2_ = bf16[1024,1024]{1,0:T(8,128)(2,1)} custom-call(bf16[1,1024,1024]{2,1,0:T(8,128)(2,1)S(1)} %copy-done.1, bf16[1,1024,1024]{2,1,0:T(8,128)(2,1)} %get-tuple-element.55.up_ref.refs_5_), custom_call_target="tpu_custom_call" | custom-call | tf_op jit(solution)/shard_map/cond/branch_1_fun/pallas_call | solution.py:29
  51.7 2.6 %collective-permute-done = bf16[128,1024]{1,0:T(8,128)(2,1)S(1)} collective-permute-done((bf16[128,1024]{1,0:T(8,128)(2,1)S(1)}, bf16[128,1024]{1,0:T(8,128)(2,1)S(1)}, u32[]{:S(2)}, u32[]{:S(2)}) %collective-permute-start) | collective-permute-done | bytes 262176 | tf_op jit(solution)/shard_map/cond/branch_1_fun/ppermute | solution.py:269
  54.4 0.0 copy-start.15
  54.4 1.5 collective-permute-start.1
  55.8 38.6 %all-gather.11.cloned.1.call-done.refs_1_ = bf16[1024,2048]{1,0:T(8,128)(2,1)} async-done(((bf16[128,2048]{1,0:T(8,128)(2,1)}), bf16[1024,2048]{1,0:T(8,128)(2,1)}) %all-gather.11.cloned.1.call-update) | async-done | bytes 4194320 | tf_op jit(solution)/shard_map/cond/branch_1_fun/all_gather | solution.py:319
  94.4 0.0 copy-done.15
  94.5 0.0 all-gather.13.cloned.1.call-update
  94.5 2.3 %constant_dynamic-slice_fusion = bf16[512,1024]{1,0:T(8,128)(2,1)} fusion(bf16[1024,1024]{1,0:T(8,128)(2,1)} %all-gather.9.cloned.1.call-done.refs_0_, s32[]{:T(128)S(6)} %select_n.115), kind=kLoop, calls=%fused_computation.5 | loop fusion | bytes 2097156 | tf_op jit(solution)/shard_map/cond/branch_1_fun/dynamic_slice | solution.py:333
  96.8 1.5 collective-permute-start.4
  98.2 0.8 and_reduce_fusion
  99.6 0.0 copy-start.3
  99.6 0.6 pad_add_fusion.flag_ref
  100.2 23.8 %collective-permute-done.4.refs_0_ = bf16[512,1024]{1,0:T(8,128)(2,1)S(1)} collective-permute-done((bf16[512,1024]{1,0:T(8,128)(2,1)}, bf16[512,1024]{1,0:T(8,128)(2,1)S(1)}, u32[]{:S(2)}, u32[]{:S(2)}) %collective-permute-start.4) | collective-permute-done | bytes 1048608 | tf_op jit(solution)/shard_map/cond/branch_1_fun/ppermute | solution.py:269
  124.0 0.0 copy-start.12
  124.0 0.0 collective-permute-start.5
  124.0 1.7 constant_dynamic-slice_fusion.1
  125.7 1.5 collective-permute-start.2
  127.2 0.0 collective-permute-done.1.refs_2_.refs_3_
  127.2 0.0 copy-done.3
  127.2 21.6 %branch_1_fun.5 = (bf16[1,1024,1024]{2,1,0:T(8,128)(2,1)}, bf16[1,1024,1024]{2,1,0:T(8,128)(2,1)}, bf16[1024,3072]{1,0:T(8,128)(2,1)}) custom-call(s32[3]{0:T(128)} %pad_add_fusion.flag_ref, bf16[1024,1024]{1,0:T(8,128)(2,1)} %all-gather.9.cloned.1.call-done.refs_0_, bf16[1024,2048]{1,0:T(8,128)(2,1)} %all-gather.11.cloned.1.call-done.refs_1_, ...), custom_call_target="tpu_custom_call" | custom-call | flops 12884901888 | bytes 25165824 | tf_op jit(solution)/shard_map/cond/branch_1_fun/pallas_call | solution.py:202
  148.8 0.0 copy-done.12
  148.8 2.2 %collective-permute-done.2.refs_0_ = bf16[512,1024]{1,0:T(8,128)(2,1)} collective-permute-done((bf16[512,1024]{1,0:T(8,128)(2,1)S(1)}, bf16[512,1024]{1,0:T(8,128)(2,1)}, u32[]{:S(2)}, u32[]{:S(2)}) %collective-permute-start.2) | collective-permute-done | bytes 1048608 | tf_op jit(solution)/shard_map/cond/branch_1_fun/ppermute | solution.py:269
  151.0 0.0 collective-permute-start.3
  151.0 0.0 collective-permute-done.5.refs_1_
  151.0 0.0 copy-start.13
  151.1 1.0 copy-done.13
  152.0 8.1 %branch_1_fun.6.refs_6_ = bf16[1024,1024]{1,0:T(8,128)(2,1)} custom-call(s32[3]{0:T(128)} %pad_add_fusion.flag_ref, bf16[512,1024]{1,0:T(8,128)(2,1)} %copy-done.12, bf16[512,1024]{1,0:T(8,128)(2,1)} %copy-done.13, bf16[1024,1024]{1,0:T(8,128)(2,1)} %collective-permute-done.1.refs_2_.refs_3_, bf16[1024,3072]{1,0:T(8,128)(2,1)} %get-tuple-element.62.refs_3_.refs_5_), custom_call_target="tpu_custom_call" | custom-call | flops 2147483648 | bytes 8388608 | tf_op jit(solution)/shard_map/cond/branch_1_fun/pallas_call | solution.py:202
  160.2 0.0 collective-permute-done.3.refs_1_
  160.2 0.0 copy-start.14
  160.2 0.0 all-gather.13.cloned.1.call-done.refs_2_
  160.2 0.9 copy-done.14
  161.1 18.5 %branch_1_fun.7 = f32[1,1024,3072]{2,1,0:T(8,128)} custom-call(s32[3]{0:T(128)} %pad_add_fusion.flag_ref, bf16[512,1024]{1,0:T(8,128)(2,1)} %collective-permute-done.2.refs_0_, bf16[512,1024]{1,0:T(8,128)(2,1)} %copy-done.14, bf16[1024,1024]{1,0:T(8,128)(2,1)} %all-gather.13.cloned.1.call-done.refs_2_, ...), custom_call_target="tpu_custom_call" | custom-call | flops 6442450944 | bytes 25165824 | tf_op jit(solution)/shard_map/cond/branch_1_fun/pallas_call | solution.py:202
  (3 shorter events, 0.0 us)
Async XLA Ops:
  10.8 34.8 %all-gather.9.cloned.1.call-start = ((), (), s32[]{:S(2)}) async-start(), calls=%async_computation.1 | async-start | bytes 2359296 | tf_op jit(solution)/shard_map/cond/branch_1_fun/all_gather | solution.py:319
  11.5 35.9 %copy-start.1 = (bf16[1,1024,1024]{2,1,0:T(8,128)(2,1)S(1)}, bf16[1,1024,1024]{2,1,0:T(8,128)(2,1)}, u32[]{:S(2)}) copy-start(bf16[1,1024,1024]{2,1,0:T(8,128)(2,1)} %get-tuple-element.54.gate_ref.refs_4_) | copy-start | bytes 6291460 | tf_op jit(solution)/shard_map/cond
  13.6 80.8 %all-gather.11.cloned.1.call-start = ((), (), s32[]{:S(2)}) async-start(), calls=%async_computation.2 | async-start | bytes 4718592 | tf_op jit(solution)/shard_map/cond/branch_1_fun/all_gather | solution.py:319
  45.6 114.6 %all-gather.13.cloned.1.call-start = ((), (), s32[]{:S(2)}) async-start(), calls=%async_computation.3 | async-start | bytes 2359296 | tf_op jit(solution)/shard_map/cond/branch_1_fun/all_gather | solution.py:319
  45.9 8.5 %collective-permute-start = (bf16[128,1024]{1,0:T(8,128)(2,1)S(1)}, bf16[128,1024]{1,0:T(8,128)(2,1)S(1)}, u32[]{:S(2)}, u32[]{:S(2)}) collective-permute-start(bf16[128,1024]{1,0:T(8,128)(2,1)S(1)} %get-tuple-element.100), channel_id=1, source_target_pairs={{0,8},{8,0},{16,24},{24,16},{1,9},{9,1},{17,25},{25,17},{2,10},{10... | collective-permute-start | bytes 786440 | tf_op jit(solution)/shard_map/cond/branch_1_fun/ppermute | solution.py:269
  54.4 40.1 %copy-start.15 = (bf16[128,1024]{1,0:T(8,128)(2,1)}, bf16[128,1024]{1,0:T(8,128)(2,1)S(1)}, u32[]{:S(2)}) copy-start(bf16[128,1024]{1,0:T(8,128)(2,1)S(1)} %collective-permute-done) | copy-start | bytes 786436 | tf_op jit(solution)/shard_map/cond
  54.4 72.8 %collective-permute-start.1 = (bf16[1024,1024]{1,0:T(8,128)(2,1)}, bf16[1024,1024]{1,0:T(8,128)(2,1)}, u32[]{:S(2)}, u32[]{:S(2)}) collective-permute-start(bf16[1024,1024]{1,0:T(8,128)(2,1)} %branch_1_fun.4.refs_2_), channel_id=1, source_target_pairs={{24,16},{16,24},{8,0},{0,8},{25,17},{17,25},{9,1},{1,9},{26,18},{1... | collective-permute-start | bytes 6291464 | tf_op jit(solution)/shard_map/cond/branch_1_fun/ppermute | solution.py:269
  96.8 27.2 %collective-permute-start.4 = (bf16[512,1024]{1,0:T(8,128)(2,1)}, bf16[512,1024]{1,0:T(8,128)(2,1)S(1)}, u32[]{:S(2)}, u32[]{:S(2)}) collective-permute-start(bf16[512,1024]{1,0:T(8,128)(2,1)} %constant_dynamic-slice_fusion), channel_id=1, source_target_pairs={{8,0},{16,24},{24,16},{0,8},{9,1},{17,25},{25,17},{1,9},{10,2},{18... | collective-permute-start | bytes 3145736 | tf_op jit(solution)/shard_map/cond/branch_1_fun/ppermute | solution.py:269
  99.6 27.6 %copy-start.3 = (bf16[1,1024,1024]{2,1,0:T(8,128)(2,1)S(1)}, bf16[1,1024,1024]{2,1,0:T(8,128)(2,1)}, u32[]{:S(2)}) copy-start(bf16[1,1024,1024]{2,1,0:T(8,128)(2,1)} %get-tuple-element.55.up_ref.refs_5_) | copy-start | bytes 6291460 | tf_op jit(solution)/shard_map/cond
  124.0 24.8 %copy-start.12 = (bf16[512,1024]{1,0:T(8,128)(2,1)}, bf16[512,1024]{1,0:T(8,128)(2,1)S(1)}, u32[]{:S(2)}) copy-start(bf16[512,1024]{1,0:T(8,128)(2,1)S(1)} %collective-permute-done.4.refs_0_) | copy-start | bytes 3145732 | tf_op jit(solution)/shard_map/cond
  124.0 27.0 %collective-permute-start.5 = (bf16[512,1024]{1,0:T(8,128)(2,1)S(1)}, bf16[512,1024]{1,0:T(8,128)(2,1)S(1)}, u32[]{:S(2)}, u32[]{:S(2)}) collective-permute-start(bf16[512,1024]{1,0:T(8,128)(2,1)S(1)} %collective-permute-done.4.refs_0_), channel_id=1, source_target_pairs={{0,1},{1,0},{2,3},{3,2},{4,5},{5,4},{6,7},{7,6},{8,9},{9,8},{10,11... | collective-permute-start | bytes 3145736 | tf_op jit(solution)/shard_map/cond/branch_1_fun/ppermute | solution.py:269
  125.7 25.4 %collective-permute-start.2 = (bf16[512,1024]{1,0:T(8,128)(2,1)S(1)}, bf16[512,1024]{1,0:T(8,128)(2,1)}, u32[]{:S(2)}, u32[]{:S(2)}) collective-permute-start(bf16[512,1024]{1,0:T(8,128)(2,1)S(1)} %constant_dynamic-slice_fusion.1), channel_id=1, source_target_pairs={{0,8},{24,16},{16,24},{8,0},{1,9},{25,17},{17,25},{9,1},{2,10},{26... | collective-permute-start | bytes 3145736 | tf_op jit(solution)/shard_map/cond/branch_1_fun/ppermute | solution.py:269
  151.0 9.1 %collective-permute-start.3 = (bf16[512,1024]{1,0:T(8,128)(2,1)}, bf16[512,1024]{1,0:T(8,128)(2,1)S(1)}, u32[]{:S(2)}, u32[]{:S(2)}) collective-permute-start(bf16[512,1024]{1,0:T(8,128)(2,1)} %collective-permute-done.2.refs_0_), channel_id=1, source_target_pairs={{7,6},{6,7},{5,4},{4,5},{3,2},{2,3},{1,0},{0,1},{15,14},{14,15},{1... | collective-permute-start | bytes 3145736 | tf_op jit(solution)/shard_map/cond/branch_1_fun/ppermute | solution.py:269
  151.0 1.0 copy-start.13
  160.2 1.0 copy-start.14
Sparse Core Ops, SparseCore 0:
  13.8 31.7 all-gather.8
  47.8 46.6 all-gather.10
  96.1 27.8 all-gather.12
where the time goes:
time: 187 us
  waiting for transfers between devices  98.4 us (53%)
  Pallas kernels  52.6 us (28%)
  between operations  15 us (8%)
  local copies, waits for them, and re-layouts  7.41 us (4%)
  starting transfers between devices  6.31 us (3%)
  other arithmetic  5.67 us (3%)
    all_gather x3, waiting for transfers between devices, gather(): return lax.all_gather(block, 'shard', axis=0, tiled=True)  69.7 us
    pallas_call x3, Pallas kernels, phase_call(): pl.pallas_call(functools.partial(phase_kernel, len(pieces), cut, wide, bl...  48.2 us
    ppermute x6, waiting for transfers between devices, send(): return lax.ppermute(value, axis, pairs[::-1] if back else pairs)  28.6 us
    ppermute x6, starting transfers between devices, send(): return lax.ppermute(value, axis, pairs[::-1] if back else pairs)  6.01 us
    pallas_call x1, Pallas kernels, hidden_transposed(): pl.pallas_call(hidden_kernel, grid=(rows // tall,), in_specs=[block, bloc...  4.35 us
    dynamic_slice x2, local copies, waits for them, and re-layouts, to_partner(): return to_slot(lax.dynamic_slice(whole, (core * half, 0), (half, width)), 1)  3.94 us
  transfers between devices with their start and end apart: 9, of which 5 were waited for; matrix products, arithmetic and copies ran while one was open for 3% of the time, Pallas kernels for 18%

commit v1 on v0

--- a/solution.py
+++ b/solution.py
@@ -36,6 +36,25 @@
     )(gate_pre, up_pre)
 
 
+def weight_kernel(master_ref, out_ref):
+    out_ref[...] = master_ref[0].astype(out_ref.dtype).T
+
+
+def weight_transposed(master):
+    _, ffw, d_model = master.shape
+    return pl.pallas_call(
+        weight_kernel,
+        grid=(ffw // tall,),
+        in_specs=[pl.BlockSpec((1, tall, d_model), lambda i: (0, i, 0))],
+        out_specs=pl.BlockSpec((d_model, tall), lambda i: (0, i)),
+        out_shape=jax.ShapeDtypeStruct((d_model, ffw), jnp.bfloat16),
+        compiler_params=params,
+        cost_estimate=pl.CostEstimate(
+            flops=0, bytes_accessed=6 * ffw * d_model, transcendentals=0
+        ),
+    )(master)
+
+
 def update_rows(master, grads, out_ref):
     square = sum(jnp.sum(g * g, axis=1, keepdims=True) for g in grads)
     scale = learn_rate / jnp.sqrt(square / master.shape[1] + rms_eps)
@@ -60,14 +79,14 @@
     refs = list(refs)
     pieces = [refs.pop(0) for _ in range(n_pieces)]
     hidden_ref = refs.pop(0) if blocks else None
-    master_hbm = refs.pop(0) if gates or update else None
+    master_hbm = refs.pop(0) if update else None
     grad_ref = refs.pop(0) if grad_in else None
     ready_ref = refs.pop(0) if ready else None
-    gate_ref, up_ref = (refs.pop(0), refs.pop(0)) if gates else (None, None)
+    weight_ref, gate_ref, up_ref = [refs.pop(0) if gates else None for _ in range(3)]
     gate_out, up_out = (refs.pop(0), refs.pop(0)) if gates else (None, None)
     out_ref = refs.pop(0) if blocks else None
     whole_ref, sem_ref = refs[:2]
-    master_ref, master_sem = refs[2:4] if gates or update else (None, None)
+    master_ref, master_sem = refs[2:4] if update else (None, None)
     sum_ref = refs[4] if update else None
     step = pl.program_id(0)
     by_block = {}
@@ -82,7 +101,7 @@
         )
         by_block.setdefault(first // wide, []).append(copy)
     master_copies = []
-    if gates or update:
+    if update:
         for i in range(master_ref.shape[0] // tall):
             lines = pl.ds(i * tall, tall)
             master_copies.append(
@@ -140,21 +159,19 @@
             if update:
                 update_rows(master_ref[lines, :], [sum_ref[lines, :]], out_ref)
             if gates:
-                weight = master_ref[lines, :].astype(jnp.bfloat16)
-                d_hidden = dot(whole_ref[...], weight, ((1,), (1,)))
+                d_hidden = dot(whole_ref[...], weight_ref[...], ((1,), (0,)))
                 gates_back(d_hidden, gate_ref, up_ref, gate_out, up_out)
 
 
 def phase_call(flags, pieces, layout, hidden=None, master=None, grad=None, gate_up=None,
-               ready=None, update=False, d_model=None, tall=256):
+               weight=None, ready=None, update=False, d_model=None):
+    ffw = hidden.shape[0] if gate_up is None else gate_up[0].shape[2]
     if master is not None:
-        _, ffw, d_model = master.shape
-    else:
-        ffw = hidden.shape[0]
+        d_model = master.shape[2]
     rows = gate_up[0].shape[1] if hidden is None else hidden.shape[1]
     wide = next(w for w in (1024, 768, 512, 128) if d_model % w == 0)
     blocks = d_model // wide if hidden is not None else 0
-    lines = ffw // tall if master is not None else 0
+    lines = ffw // tall if update or gate_up is not None else 0
     cut = []
     for ref, index, row, first, count in layout:
         piece = wide if blocks else count
@@ -187,8 +204,8 @@
         specs.append(pl.BlockSpec((ffw, wide), lambda i, flag: (0, 0)))
         args.append(ready)
     if gate_up is not None:
-        specs += [side, side]
-        args += list(gate_up)
+        specs += [pl.BlockSpec((d_model, tall), lambda i, flag: (0, row_block(i))), side, side]
+        args += [weight, *gate_up]
         out_specs += [side, side]
         out_shape += [jax.ShapeDtypeStruct(a.shape, a.dtype) for a in gate_up]
     if update:
@@ -235,7 +252,7 @@
         in_specs=[full] + [part] * len(grads),
         out_specs=full,
         out_shape=jax.ShapeDtypeStruct(master.shape, master.dtype),
-        compiler_params=params,
+        compiler_params=pltpu.CompilerParams(vmem_limit_bytes=20 * 2**20),
     )(master, *grads)
 
 
@@ -291,7 +308,7 @@
         three = jnp.where(chip == 0, end, three)
         return [block, one, two, three]
 
-    def all_sum(grad):
+    def all_sum(grad, held):
         half = grad.shape[0] // 2
         done = []
         for part, bits in ((grad[:half], (1, 2)), (grad[half:], (2, 1))):
@@ -302,6 +319,7 @@
                 send = lax.dynamic_slice_in_dim(part, (1 - side) * high, high)
                 got = to_slot(send, bit)
                 part = (keep.astype(jnp.float32) + got.astype(jnp.float32)).astype(part.dtype)
+            part = after(part, held)
             for bit, side in zip(bits[::-1], sides[::-1]):
                 got = to_slot(part, bit)
                 part = jnp.concatenate(
@@ -332,13 +350,14 @@
             def to_partner(whole):
                 return to_slot(lax.dynamic_slice(whole, (core * half, 0), (half, width)), 1)
 
-            first = to_partner(one)
+            weight = weight_transposed(master)
+            first = to_partner(after(one, weight))
             second = to_partner(two)
             flags = jnp.stack([share(1).astype(jnp.int32), core * half, (1 - core) * half])
             layout = [(0, None, 0, 0, width), (1, None, 0, width, 2 * width)]
             d_gate, d_up, grad = phase_call(
-                flags, after([one, two], theirs), layout, hidden, master, gate_up=gate_up,
-                tall=512,
+                flags, after([one, two], theirs), layout, hidden, gate_up=gate_up, weight=weight,
+                d_model=d_model,
             )
             layout = [(0, None, (1,), 0, width), (1, None, (2,), 0, width)]
             ready = phase_call(
@@ -356,30 +375,35 @@
             )[0]
             return d_gate, d_up, fresh
         hidden = hidden_transposed(gate_pre, up_pre)
+        weight = weight_transposed(master)
         flags = jnp.zeros((1,), jnp.int32)
         if mode == "none":
             layout = [(0, None, 0, 0, d_model)]
             return tuple(
                 phase_call(
-                    flags, [gather(masked)], layout, hidden, master, gate_up=gate_up, update=True
+                    flags, [gather(masked)], layout, hidden, master, gate_up=gate_up,
+                    weight=weight, update=True,
                 )
             )
-        half = d_model // 2
-        one = gather(masked[:, :half])
-        two = gather(after(masked[:, half:], one))
-        layout = [(0, None, 0, 0, half)]
-        grads = []
-        for whole in (one, two):
-            grad = phase_call(flags, [whole], layout, hidden, d_model=half)[0]
+        width = d_model // 3
+        wholes, grads = [], []
+        for first in range(0, d_model, width):
+            block = masked[:, first : first + width]
+            wholes.append(gather(after(block, wholes[-1]) if wholes else block))
+            layout = [(0, None, 0, 0, width)]
+            grads.append(phase_call(flags, wholes[-1:], layout, hidden, d_model=width)[0])
+        layout = [(i, None, 0, i * width, width) for i in range(3)]
+        d_gate, d_up = phase_call(
+            flags, wholes, layout, gate_up=gate_up, weight=weight, d_model=d_model
+        )
+        held = grads[1:] + [d_gate]
+        for i, grad in enumerate(grads):
             if mode == "four":
-                grad = all_sum(grad)
-            else:
-                for bit in (1, 2):
-                    got = to_slot(grad, bit)
-                    grad = grad + jnp.where(share(bit), got, jnp.zeros((), got.dtype))
-            grads.append(grad)
-        layout = layout + [(1, None, 0, half, half)]
-        d_gate, d_up = phase_call(flags, [one, two], layout, master=master, gate_up=gate_up, tall=512)
+                grads[i] = all_sum(grad, held[i])
+                continue
+            for bit in (1, 2):
+                got = to_slot(grads[i], bit)
+                grads[i] = grads[i] + jnp.where(share(bit), got, jnp.zeros((), got.dtype))
         return d_gate, d_up, update_call(master, grads)
 
     modes = ["none", "pair", "four"] + (["mixed"] if n_slot > 4 else [])

time: 187 us -> 214 us (1.14)
  starting transfers between devices: 6.31 us -> 26.4 us
  other arithmetic: 5.67 us -> 13.5 us
  waiting for transfers between devices: 98.4 us -> 94.1 us
  local copies, waits for them, and re-layouts: 7.41 us -> 10.6 us
    all_gather x3, waiting for transfers between devices: 69.7 us -> 31.9 us  [gather(): return lax.all_gather(block, 'shard', axis=0, tiled=True)]
    ppermute x6 -> x24, waiting for transfers between devices: 28.6 us -> 62.1 us  [send(): return lax.ppermute(value, axis, pairs[::-1] if back else pairs)]
    ppermute x6 -> x24, starting transfers between devices: 6.01 us -> 26.3 us  [send(): return lax.ppermute(value, axis, pairs[::-1] if back else pairs)]
    pallas_call x0 -> x2, Pallas kernels: none -> 14.4 us  [the longest x1 7.89 us: weight_transposed(): pl.pallas_call(weight_kernel, grid=(ffw // tall,), in_specs=[pl.BlockSpec...]
    pallas_call x3 -> x4, Pallas kernels: 48.2 us -> 34.1 us  [phase_call(): pl.pallas_call(functools.partial(phase_kernel, len(pieces), cut, wide, bl...]
    convert_element_type x0 -> x12, other arithmetic: none -> 5.41 us  [all_sum(): (keep.astype(jnp.float32) + got.astype(jnp.float32)).astype(part.dtype)]
    slice x2 -> x4, local copies, waits for them, and re-layouts: 1.57 us -> 6.18 us  [the longest x3 5.29 us: all_sum(): grad[:half]]
    select_n x0 -> x12, other arithmetic: none -> 2.8 us  [all_sum(): jnp.where(side == 0, part, got)]
  transfers between devices with their start and end apart: 9 -> 27, of which waited for: 5 -> 14; matrix products, arithmetic and copies ran while one was open for 3% -> 7% of each run, Pallas kernels for 18% -> 19%
where the time goes in v1:
time: 214 us; the launch traced here: 213 us
  waiting for transfers between devices  94.1 us (44%)
  Pallas kernels  52.9 us (25%)
  starting transfers between devices  26.4 us (12%)
  between operations  15 us (7%)
  other arithmetic  13.5 us (6%)
  local copies, waits for them, and re-layouts  10.6 us (5%)
    ppermute x24, waiting for transfers between devices, send(): return lax.ppermute(value, axis, pairs[::-1] if back else pairs)  62.1 us
    pallas_call x4, Pallas kernels, phase_call(): pl.pallas_call(functools.partial(phase_kernel, len(pieces), cut, wide, bl...  34.1 us
    all_gather x3, waiting for transfers between devices, gather(): return lax.all_gather(block, 'shard', axis=0, tiled=True)  31.9 us
    ppermute x24, starting transfers between devices, send(): return lax.ppermute(value, axis, pairs[::-1] if back else pairs)  26.3 us
    pallas_call x1, Pallas kernels, weight_transposed(): pl.pallas_call(weight_kernel, grid=(ffw // tall,), in_specs=[pl.BlockSpec...  7.89 us
    pallas_call x1, Pallas kernels, update_call(): pl.pallas_call(update_kernel, grid=(ffw // 128,), in_specs=[full] + [part...  6.52 us
    convert_element_type x12, other arithmetic, all_sum(): (keep.astype(jnp.float32) + got.astype(jnp.float32)).astype(part.dtype)  5.41 us
    slice x3, local copies, waits for them, and re-layouts, all_sum(): grad[:half]  5.29 us
  transfers between devices with their start and end apart: 27, of which 14 were waited for; matrix products, arithmetic and copies ran while one was open for 7% of the time, Pallas kernels for 19%

profile of v1, /device:TPU:0, one launch (start us, length us, event | category | flops | bytes accessed | tf_op | source)
XLA Modules:
  0.0 213.4 jit_solution(18252641920157279018)
XLA Ops:
  8.0 1.4 convert_reduce_fusion
  10.7 196.1 %conditional.1 = ((bf16[1,1024,1024]{2,1,0:T(8,128)(2,1)}, bf16[1,1024,1024]{2,1,0:T(8,128)(2,1)}, f32[1,1024,3072]{2,1,0:T(8,128)})) conditional(s32[]{:T(128)} %clamp.3, (s32[1,1]{1,0:T(1,128)}, bf16[1,128,3072]{2,1,0:T(8,128)(2,1)}, bf16[1,1024,1024]{2,1,0:T(8,128)(2,1)}, bf16[1,1024,1024]{2,1,0:T(8,128)(2,1)}, ...), branch_computations={%region_2.3_spmd, %region_3.5_spmd, %region_5.6_spmd} | conditional | flops 21475229696 | bytes 277612640 | solution.py:412
  11.8 1.3 bitcast_select_fusion.2
  14.1 31.9 %all-gather.16.cloned.1.call-done.refs_0_ = bf16[1024,1024]{1,0:T(8,128)(2,1)} async-done(((bf16[128,1024]{1,0:T(8,128)(2,1)}), bf16[1024,1024]{1,0:T(8,128)(2,1)}) %all-gather.16.cloned.1.call-update) | async-done | bytes 2097168 | tf_op jit(solution)/shard_map/cond/branch_2_fun/all_gather | solution.py:337
  46.1 4.4 %branch_2_fun.9.refs_1_ = bf16[1024,1024]{1,0:T(8,128)(2,1)} custom-call(bf16[1,1024,1024]{2,1,0:T(8,128)(2,1)S(1)} %copy-done.2, bf16[1,1024,1024]{2,1,0:T(8,128)(2,1)} %get-tuple-element.72.refs_5_.up_ref), custom_call_target="tpu_custom_call" | custom-call | tf_op jit(solution)/shard_map/cond/branch_2_fun/pallas_call | solution.py:29
  50.4 6.9 %branch_2_fun.10 = bf16[1024,1024]{1,0:T(8,128)(2,1)} custom-call(s32[1]{0:T(128)} %constant.29.clone.flag_ref, bf16[1024,1024]{1,0:T(8,128)(2,1)} %all-gather.16.cloned.1.call-done.refs_0_, bf16[1024,1024]{1,0:T(8,128)(2,1)} %branch_2_fun.9.refs_1_), custom_call_target="tpu_custom_call" | custom-call | flops 2147483648 | bytes 8388608 | tf_op jit(solution)/shard_map/cond/branch_2_fun/pallas_call | solution.py:219
  57.3 1.7 fusion.5
  59.1 1.5 collective-permute-start.10
  61.4 1.5 collective-permute-start.6
  62.9 10.3 %collective-permute-done.10 = bf16[256,1024]{1,0:T(8,128)(2,1)S(1)} collective-permute-done((bf16[256,1024]{1,0:T(8,128)(2,1)S(1)}, bf16[256,1024]{1,0:T(8,128)(2,1)S(1)}, u32[]{:S(2)}, u32[]{:S(2)}) %collective-permute-start.10) | collective-permute-done | bytes 524320 | tf_op jit(solution)/shard_map/cond/branch_2_fun/ppermute | solution.py:286
  73.4 1.5 collective-permute-start.11
  75.5 1.2 add_convert_fusion.5
  77.8 7.9 %branch_2_fun.7.refs_3_ = bf16[3072,1024]{1,0:T(8,128)(2,1)} custom-call(f32[1,1024,3072]{2,1,0:T(8,128)} %get-tuple-element.70.master_ref), custom_call_target="tpu_custom_call" | custom-call | bytes 18874368 | tf_op jit(solution)/shard_map/cond/branch_2_fun/pallas_call | solution.py:45
  85.9 6.8 %branch_2_fun.11 = bf16[1024,1024]{1,0:T(8,128)(2,1)} custom-call(s32[1]{0:T(128)} %constant.29.clone.flag_ref, bf16[1024,1024]{1,0:T(8,128)(2,1)} %all-gather.18.cloned.1.call-done.refs_1_.refs_0_, bf16[1024,1024]{1,0:T(8,128)(2,1)} %branch_2_fun.9.refs_1_), custom_call_target="tpu_custom_call" | custom-call | flops 2147483648 | bytes 8388608 | tf_op jit(solution)/shard_map/cond/branch_2_fun/pallas_call | solution.py:219
  92.7 1.2 collective-permute-start.12
  93.9 1.7 fusion.4
  95.6 1.5 collective-permute-start.8
  97.9 1.0 collective-permute-start.14
  98.9 2.4 %collective-permute-done.12 = bf16[128,1024]{1,0:T(8,128)(2,1)S(1)} collective-permute-done((bf16[128,1024]{1,0:T(8,128)(2,1)S(1)}, bf16[128,1024]{1,0:T(8,128)(2,1)S(1)}, u32[]{:S(2)}, u32[]{:S(2)}) %collective-permute-start.12) | collective-permute-done | bytes 262176 | tf_op jit(solution)/shard_map/cond/branch_2_fun/ppermute | solution.py:286
  101.9 3.0 %collective-permute-done.8 = bf16[128,1024]{1,0:T(8,128)(2,1)S(1)} collective-permute-done((bf16[128,1024]{1,0:T(8,128)(2,1)S(1)}, bf16[128,1024]{1,0:T(8,128)(2,1)S(1)}, u32[]{:S(2)}, u32[]{:S(2)}) %collective-permute-start.8) | collective-permute-done | bytes 262176 | tf_op jit(solution)/shard_map/cond/branch_2_fun/ppermute | solution.py:286
  105.0 1.0 collective-permute-start.9
  106.0 10.1 %collective-permute-done.18 = bf16[256,1024]{1,0:T(8,128)(2,1)S(1)} collective-permute-done((bf16[256,1024]{1,0:T(8,128)(2,1)S(1)}, bf16[256,1024]{1,0:T(8,128)(2,1)S(1)}, u32[]{:S(2)}, u32[]{:S(2)}) %collective-permute-start.18) | collective-permute-done | bytes 524320 | tf_op jit(solution)/shard_map/cond/branch_2_fun/ppermute | solution.py:286
  116.4 1.0 collective-permute-start.19
  117.6 1.3 collective-permute-start.15
  118.9 8.5 %collective-permute-done.13 = bf16[256,1024]{1,0:T(8,128)(2,1)S(1)} collective-permute-done((bf16[256,1024]{1,0:T(8,128)(2,1)S(1)}, bf16[256,1024]{1,0:T(8,128)(2,1)S(1)}, u32[]{:S(2)}, u32[]{:S(2)}) %collective-permute-start.13) | collective-permute-done | bytes 524320 | tf_op jit(solution)/shard_map/cond/branch_2_fun/ppermute | solution.py:286
  128.9 1.8 collective-permute-done.15
  130.8 6.8 %branch_2_fun.12 = bf16[1024,1024]{1,0:T(8,128)(2,1)} custom-call(s32[1]{0:T(128)} %constant.29.clone.flag_ref, bf16[1024,1024]{1,0:T(8,128)(2,1)} %all-gather.20.cloned.1.call-done.refs_2_.refs_0_, bf16[1024,1024]{1,0:T(8,128)(2,1)} %branch_2_fun.9.refs_1_), custom_call_target="tpu_custom_call" | custom-call | flops 2147483648 | bytes 8388608 | tf_op jit(solution)/shard_map/cond/branch_2_fun/pallas_call | solution.py:219
  137.7 1.9 fusion.3
  139.6 1.0 collective-permute-start.20
  143.3 1.1 collective-permute-start.26
  144.4 1.1 collective-permute-start.22
  145.5 13.6 %branch_2_fun.8 = (bf16[1,1024,1024]{2,1,0:T(8,128)(2,1)}, bf16[1,1024,1024]{2,1,0:T(8,128)(2,1)}) custom-call(s32[1]{0:T(128)} %constant.29.clone.flag_ref, bf16[1024,1024]{1,0:T(8,128)(2,1)} %all-gather.16.cloned.1.call-done.refs_0_, bf16[1024,1024]{1,0:T(8,128)(2,1)} %all-gather.18.cloned.1.call-done.refs_1_.refs_0_, ...), custom_call_target="tpu_custom_call" | custom-call | flops 6442450944 | bytes 25165824 | tf_op jit(solution)/shard_map/cond/branch_2_fun/pallas_call | solution.py:219
  159.1 1.1 broadcast_select_fusion.15
  160.2 1.5 collective-permute-start.21
  161.7 1.2 add_convert_fusion
  163.6 1.2 add_convert_fusion.1
  164.9 1.1 collective-permute-start.23
  166.1 1.1 collective-permute-start.17
  167.2 5.1 %collective-permute-done.27 = bf16[128,1024]{1,0:T(8,128)(2,1)S(1)} collective-permute-done((bf16[128,1024]{1,0:T(8,128)(2,1)S(1)}, bf16[128,1024]{1,0:T(8,128)(2,1)S(1)}, u32[]{:S(2)}, u32[]{:S(2)}) %collective-permute-start.27) | collective-permute-done | bytes 262176 | tf_op jit(solution)/shard_map/cond/branch_2_fun/ppermute | solution.py:286
  172.4 5.4 %collective-permute-done.23 = bf16[128,1024]{1,0:T(8,128)(2,1)S(1)} collective-permute-done((bf16[128,1024]{1,0:T(8,128)(2,1)S(1)}, bf16[128,1024]{1,0:T(8,128)(2,1)S(1)}, u32[]{:S(2)}, u32[]{:S(2)}) %collective-permute-start.23) | collective-permute-done | bytes 262176 | tf_op jit(solution)/shard_map/cond/branch_2_fun/ppermute | solution.py:286
  177.9 1.5 collective-permute-start.24
  180.2 4.2 %collective-permute-done.24 = bf16[128,1024]{1,0:T(8,128)(2,1)S(1)} collective-permute-done((bf16[128,1024]{1,0:T(8,128)(2,1)S(1)}, bf16[128,1024]{1,0:T(8,128)(2,1)S(1)}, u32[]{:S(2)}, u32[]{:S(2)}) %collective-permute-start.24) | collective-permute-done | bytes 262176 | tf_op jit(solution)/shard_map/cond/branch_2_fun/ppermute | solution.py:286
  184.5 1.5 collective-permute-start.25
  186.0 2.6 %collective-permute-done.28 = bf16[128,1024]{1,0:T(8,128)(2,1)S(1)} collective-permute-done((bf16[128,1024]{1,0:T(8,128)(2,1)S(1)}, bf16[128,1024]{1,0:T(8,128)(2,1)S(1)}, u32[]{:S(2)}, u32[]{:S(2)}) %collective-permute-start.28) | collective-permute-done | bytes 262176 | tf_op jit(solution)/shard_map/cond/branch_2_fun/ppermute | solution.py:286
  189.6 6.6 %collective-permute-done.25 = bf16[256,1024]{1,0:T(8,128)(2,1)S(1)} collective-permute-done((bf16[256,1024]{1,0:T(8,128)(2,1)S(1)}, bf16[256,1024]{1,0:T(8,128)(2,1)S(1)}, u32[]{:S(2)}, u32[]{:S(2)}) %collective-permute-start.25) | collective-permute-done | bytes 524320 | tf_op jit(solution)/shard_map/cond/branch_2_fun/ppermute | solution.py:286
  196.4 1.4 collective-permute-done.29
  198.8 1.5 slice-done.2
  200.3 6.5 %branch_2_fun.13 = f32[1,1024,3072]{2,1,0:T(8,128)} custom-call(f32[1,1024,3072]{2,1,0:T(8,128)S(1)} %bitcast.13, bf16[1024,1024]{1,0:T(8,128)(2,1)S(1)} %pad_maximum_fusion.refs_0_, bf16[1024,1024]{1,0:T(8,128)(2,1)S(1)} %get-tuple-element.145.refs_1_, bf16[1024,1024]{1,0:T(8,128)(2,1)S(1)} %get-tuple-element.146.refs_2_), custom_call_target="tpu_custom_call" | custom-call | tf_op jit(solution)/shard_map/cond/branch_2_fun/pallas_call | solution.py:249
  (90 shorter events, 15.7 us)
Async XLA Ops:
  11.0 35.1 %copy-start.2 = (bf16[1,1024,1024]{2,1,0:T(8,128)(2,1)S(1)}, bf16[1,1024,1024]{2,1,0:T(8,128)(2,1)}, u32[]{:S(2)}) copy-start(bf16[1,1024,1024]{2,1,0:T(8,128)(2,1)} %get-tuple-element.71.refs_4_.gate_ref) | copy-start | bytes 6291460 | tf_op jit(solution)/shard_map/cond
  11.0 35.0 %all-gather.16.cloned.1.call-start = ((), (), s32[]{:S(2)}) async-start(), calls=%async_computation.4 | async-start | bytes 2359296 | tf_op jit(solution)/shard_map/cond/branch_2_fun/all_gather | solution.py:337
  14.0 71.8 %all-gather.18.cloned.1.call-start = ((), (), s32[]{:S(2)}) async-start(), calls=%async_computation.5 | async-start | bytes 2359296 | tf_op jit(solution)/shard_map/cond/branch_2_fun/all_gather | solution.py:337
  46.0 84.8 %all-gather.20.cloned.1.call-start = ((), (), s32[]{:S(2)}) async-start(), calls=%async_computation.6 | async-start | bytes 2359296 | tf_op jit(solution)/shard_map/cond/branch_2_fun/all_gather | solution.py:337
  59.1 14.1 %collective-permute-start.10 = (bf16[256,1024]{1,0:T(8,128)(2,1)S(1)}, bf16[256,1024]{1,0:T(8,128)(2,1)S(1)}, u32[]{:S(2)}, u32[]{:S(2)}) collective-permute-start(bf16[256,1024]{1,0:T(8,128)(2,1)S(1)} %constant_dynamic-slice_fusion.11), channel_id=1, source_target_pairs={{8,24},{16,0},{24,8},{0,16},{9,25},{17,1},{25,9},{1,17},{10,26},{1... | collective-permute-start | bytes 1572872 | tf_op jit(solution)/shard_map/cond/branch_2_fun/ppermute | solution.py:286
  61.4 14.1 %collective-permute-start.6 = (bf16[256,1024]{1,0:T(8,128)(2,1)}, bf16[256,1024]{1,0:T(8,128)(2,1)}, u32[]{:S(2)}, u32[]{:S(2)}) collective-permute-start(bf16[256,1024]{1,0:T(8,128)(2,1)} %constant_dynamic-slice_fusion.13), channel_id=1, source_target_pairs={{0,8},{8,0},{16,24},{24,16},{1,9},{9,1},{17,25},{25,17},{2,10},{10... | collective-permute-start | bytes 1572872 | tf_op jit(solution)/shard_map/cond/branch_2_fun/ppermute | solution.py:286
  73.4 12.2 %collective-permute-start.11 = (bf16[128,1024]{1,0:T(8,128)(2,1)S(1)}, bf16[128,1024]{1,0:T(8,128)(2,1)S(1)}, u32[]{:S(2)}, u32[]{:S(2)}) collective-permute-start(bf16[128,1024]{1,0:T(8,128)(2,1)S(1)} %constant_dynamic-slice_fusion.10), channel_id=1, source_target_pairs={{8,0},{16,24},{24,16},{0,8},{9,1},{17,25},{25,17},{1,9},{10,2},{18... | collective-permute-start | bytes 786440 | tf_op jit(solution)/shard_map/cond/branch_2_fun/ppermute | solution.py:286
  76.8 9.0 %collective-permute-start.7 = (bf16[128,1024]{1,0:T(8,128)(2,1)S(1)}, bf16[128,1024]{1,0:T(8,128)(2,1)S(1)}, u32[]{:S(2)}, u32[]{:S(2)}) collective-permute-start(bf16[128,1024]{1,0:T(8,128)(2,1)S(1)} %constant_dynamic-slice_fusion.12), channel_id=1, source_target_pairs={{0,16},{8,24},{16,0},{24,8},{1,17},{9,25},{17,1},{25,9},{2,18},{10... | collective-permute-start | bytes 786440 | tf_op jit(solution)/shard_map/cond/branch_2_fun/ppermute | solution.py:286
  92.7 8.5 %collective-permute-start.12 = (bf16[128,1024]{1,0:T(8,128)(2,1)S(1)}, bf16[128,1024]{1,0:T(8,128)(2,1)S(1)}, u32[]{:S(2)}, u32[]{:S(2)}) collective-permute-start(bf16[128,1024]{1,0:T(8,128)(2,1)S(1)} %add_convert_fusion.10), channel_id=1, source_target_pairs={{0,8},{24,16},{16,24},{8,0},{1,9},{25,17},{17,25},{9,1},{2,10},{26... | collective-permute-start | bytes 786440 | tf_op jit(solution)/shard_map/cond/branch_2_fun/ppermute | solution.py:286
  95.6 9.3 %collective-permute-start.8 = (bf16[128,1024]{1,0:T(8,128)(2,1)S(1)}, bf16[128,1024]{1,0:T(8,128)(2,1)S(1)}, u32[]{:S(2)}, u32[]{:S(2)}) collective-permute-start(bf16[128,1024]{1,0:T(8,128)(2,1)S(1)} %add_convert_fusion.11), channel_id=1, source_target_pairs={{24,8},{16,0},{8,24},{0,16},{25,9},{17,1},{9,25},{1,17},{26,10},{1... | collective-permute-start | bytes 786440 | tf_op jit(solution)/shard_map/cond/branch_2_fun/ppermute | solution.py:286
  97.2 19.0 %collective-permute-start.18 = (bf16[256,1024]{1,0:T(8,128)(2,1)S(1)}, bf16[256,1024]{1,0:T(8,128)(2,1)S(1)}, u32[]{:S(2)}, u32[]{:S(2)}) collective-permute-start(bf16[256,1024]{1,0:T(8,128)(2,1)S(1)} %constant_dynamic-slice_fusion.7), channel_id=1, source_target_pairs={{24,8},{0,16},{8,24},{16,0},{25,9},{1,17},{9,25},{17,1},{26,10},{2... | collective-permute-start | bytes 1572872 | tf_op jit(solution)/shard_map/cond/branch_2_fun/ppermute | solution.py:286
  97.9 19.6 %collective-permute-start.14 = (bf16[256,1024]{1,0:T(8,128)(2,1)S(1)}, bf16[256,1024]{1,0:T(8,128)(2,1)S(1)}, u32[]{:S(2)}, u32[]{:S(2)}) collective-permute-start(bf16[256,1024]{1,0:T(8,128)(2,1)S(1)} %constant_dynamic-slice_fusion.9), channel_id=1, source_target_pairs={{16,24},{24,16},{0,8},{8,0},{17,25},{25,17},{1,9},{9,1},{18,26},{2... | collective-permute-start | bytes 1572872 | tf_op jit(solution)/shard_map/cond/branch_2_fun/ppermute | solution.py:286
  101.3 26.1 %collective-permute-start.13 = (bf16[256,1024]{1,0:T(8,128)(2,1)S(1)}, bf16[256,1024]{1,0:T(8,128)(2,1)S(1)}, u32[]{:S(2)}, u32[]{:S(2)}) collective-permute-start(bf16[256,1024]{1,0:T(8,128)(2,1)S(1)} %pad_maximum_fusion.4), channel_id=1, source_target_pairs={{0,16},{24,8},{16,0},{8,24},{1,17},{25,9},{17,1},{9,25},{2,18},{26... | collective-permute-start | bytes 1572872 | tf_op jit(solution)/shard_map/cond/branch_2_fun/ppermute | solution.py:286
  105.0 22.6 %collective-permute-start.9 = (bf16[256,1024]{1,0:T(8,128)(2,1)S(1)}, bf16[256,1024]{1,0:T(8,128)(2,1)S(1)}, u32[]{:S(2)}, u32[]{:S(2)}) collective-permute-start(bf16[256,1024]{1,0:T(8,128)(2,1)S(1)} %pad_maximum_fusion.3), channel_id=1, source_target_pairs={{24,16},{16,24},{8,0},{0,8},{25,17},{17,25},{9,1},{1,9},{26,18},{1... | collective-permute-start | bytes 1572872 | tf_op jit(solution)/shard_map/cond/branch_2_fun/ppermute | solution.py:286
  116.4 11.7 %collective-permute-start.19 = (bf16[128,1024]{1,0:T(8,128)(2,1)S(1)}, bf16[128,1024]{1,0:T(8,128)(2,1)S(1)}, u32[]{:S(2)}, u32[]{:S(2)}) collective-permute-start(bf16[128,1024]{1,0:T(8,128)(2,1)S(1)} %constant_dynamic-slice_fusion.6), channel_id=1, source_target_pairs={{24,16},{0,8},{8,0},{16,24},{25,17},{1,9},{9,1},{17,25},{26,18},{2... | collective-permute-start | bytes 786440 | tf_op jit(solution)/shard_map/cond/branch_2_fun/ppermute | solution.py:286
  117.6 13.1 %collective-permute-start.15 = (bf16[128,1024]{1,0:T(8,128)(2,1)S(1)}, bf16[128,1024]{1,0:T(8,128)(2,1)S(1)}, u32[]{:S(2)}, u32[]{:S(2)}) collective-permute-start(bf16[128,1024]{1,0:T(8,128)(2,1)S(1)} %constant_dynamic-slice_fusion.8), channel_id=1, source_target_pairs={{16,0},{24,8},{0,16},{8,24},{17,1},{25,9},{1,17},{9,25},{18,2},{26... | collective-permute-start | bytes 786440 | tf_op jit(solution)/shard_map/cond/branch_2_fun/ppermute | solution.py:286
  137.7 1.9 copy-start.11
  137.7 7.8 %copy-start.6 = (bf16[1,1024,1024]{2,1,0:T(8,128)(2,1)S(1)}, bf16[1,1024,1024]{2,1,0:T(8,128)(2,1)}, u32[]{:S(2)}) copy-start(bf16[1,1024,1024]{2,1,0:T(8,128)(2,1)} %get-tuple-element.72.refs_5_.up_ref) | copy-start | bytes 6291460 | tf_op jit(solution)/shard_map/cond
  139.6 2.9 %copy-start.7 = (bf16[512,1024]{1,0:T(8,128)(2,1)}, bf16[512,1024]{1,0:T(8,128)(2,1)S(1)}, u32[]{:S(2)}) copy-start(bf16[512,1024]{1,0:T(8,128)(2,1)S(1)} %get-tuple-element.113) | copy-start | bytes 3145732 | tf_op jit(solution)/shard_map/cond
  139.6 5.9 %copy-start.3 = (bf16[1,1024,1024]{2,1,0:T(8,128)(2,1)S(1)}, bf16[1,1024,1024]{2,1,0:T(8,128)(2,1)}, u32[]{:S(2)}) copy-start(bf16[1,1024,1024]{2,1,0:T(8,128)(2,1)} %get-tuple-element.71.refs_4_.gate_ref) | copy-start | bytes 6291460 | tf_op jit(solution)/shard_map/cond
  139.6 19.5 %collective-permute-start.20 = (bf16[128,1024]{1,0:T(8,128)(2,1)S(1)}, bf16[128,1024]{1,0:T(8,128)(2,1)}, u32[]{:S(2)}, u32[]{:S(2)}) collective-permute-start(bf16[128,1024]{1,0:T(8,128)(2,1)S(1)} %copy-done.11), channel_id=1, source_target_pairs={{16,24},{8,0},{0,8},{24,16},{17,25},{9,1},{1,9},{25,17},{18,26},{1... | collective-permute-start | bytes 786440 | tf_op jit(solution)/shard_map/cond/branch_2_fun/ppermute | solution.py:286
  140.6 21.0 %collective-permute-start.16 = (bf16[128,1024]{1,0:T(8,128)(2,1)S(1)}, bf16[128,1024]{1,0:T(8,128)(2,1)S(1)}, u32[]{:S(2)}, u32[]{:S(2)}) collective-permute-start(bf16[128,1024]{1,0:T(8,128)(2,1)S(1)} %add_convert_fusion.9), channel_id=1, source_target_pairs={{8,24},{0,16},{24,8},{16,0},{9,25},{1,17},{25,9},{17,1},{10,26},{2... | collective-permute-start | bytes 786440 | tf_op jit(solution)/shard_map/cond/branch_2_fun/ppermute | solution.py:286
  143.3 18.4 %collective-permute-start.26 = (bf16[256,1024]{1,0:T(8,128)(2,1)}, bf16[256,1024]{1,0:T(8,128)(2,1)}, u32[]{:S(2)}, u32[]{:S(2)}) collective-permute-start(bf16[256,1024]{1,0:T(8,128)(2,1)} %constant_dynamic-slice_fusion.3), channel_id=1, source_target_pairs={{0,16},{8,24},{16,0},{24,8},{1,17},{9,25},{17,1},{25,9},{2,18},{10... | collective-permute-start | bytes 1572872 | tf_op jit(solution)/shard_map/cond/branch_2_fun/ppermute | solution.py:286
  144.4 19.2 %collective-permute-start.22 = (bf16[256,1024]{1,0:T(8,128)(2,1)}, bf16[256,1024]{1,0:T(8,128)(2,1)}, u32[]{:S(2)}, u32[]{:S(2)}) collective-permute-start(bf16[256,1024]{1,0:T(8,128)(2,1)} %constant_dynamic-slice_fusion.5), channel_id=1, source_target_pairs={{0,8},{8,0},{16,24},{24,16},{1,9},{9,1},{17,25},{25,17},{2,10},{10... | collective-permute-start | bytes 1572872 | tf_op jit(solution)/shard_map/cond/branch_2_fun/ppermute | solution.py:286
  159.1 2.7 %copy-start.8 = (bf16[512,1024]{1,0:T(8,128)(2,1)S(1)}, bf16[512,1024]{1,0:T(8,128)(2,1)}, u32[]{:S(2)}) copy-start(bf16[512,1024]{1,0:T(8,128)(2,1)} %copy-done.7) | copy-start | bytes 3145732 | tf_op jit(solution)/shard_map/cond
  160.2 19.7 %collective-permute-start.21 = (bf16[256,1024]{1,0:T(8,128)(2,1)S(1)}, bf16[256,1024]{1,0:T(8,128)(2,1)S(1)}, u32[]{:S(2)}, u32[]{:S(2)}) collective-permute-start(bf16[256,1024]{1,0:T(8,128)(2,1)S(1)} %pad_maximum_fusion.6), channel_id=1, source_target_pairs={{16,0},{8,24},{0,16},{24,8},{17,1},{9,25},{1,17},{25,9},{18,2},{10... | collective-permute-start | bytes 1572872 | tf_op jit(solution)/shard_map/cond/branch_2_fun/ppermute | solution.py:286
  163.0 9.3 %collective-permute-start.27 = (bf16[128,1024]{1,0:T(8,128)(2,1)S(1)}, bf16[128,1024]{1,0:T(8,128)(2,1)S(1)}, u32[]{:S(2)}, u32[]{:S(2)}) collective-permute-start(bf16[128,1024]{1,0:T(8,128)(2,1)S(1)} %constant_dynamic-slice_fusion.2), channel_id=1, source_target_pairs={{0,8},{8,0},{16,24},{24,16},{1,9},{9,1},{17,25},{25,17},{2,10},{10... | collective-permute-start | bytes 786440 | tf_op jit(solution)/shard_map/cond/branch_2_fun/ppermute | solution.py:286
  164.9 34.0 %slice-start = ((s8[12582912]{0:T(1024)(128)(4,1)}), s8[4194304]{0:T(1024)(128)(4,1)S(1)}, s32[]{:S(2)}) async-start(s8[12582912]{0:T(1024)(128)(4,1)} %bitcast.12), calls=%async_computation.7 | async-start | bytes 8388608 | tf_op jit(solution)/shard_map/cond
  164.9 12.9 %collective-permute-start.23 = (bf16[128,1024]{1,0:T(8,128)(2,1)S(1)}, bf16[128,1024]{1,0:T(8,128)(2,1)S(1)}, u32[]{:S(2)}, u32[]{:S(2)}) collective-permute-start(bf16[128,1024]{1,0:T(8,128)(2,1)S(1)} %constant_dynamic-slice_fusion.4), channel_id=1, source_target_pairs={{0,16},{8,24},{16,0},{24,8},{1,17},{9,25},{17,1},{25,9},{2,18},{10... | collective-permute-start | bytes 786440 | tf_op jit(solution)/shard_map/cond/branch_2_fun/ppermute | solution.py:286
  166.1 23.3 %collective-permute-start.17 = (bf16[256,1024]{1,0:T(8,128)(2,1)S(1)}, bf16[256,1024]{1,0:T(8,128)(2,1)S(1)}, u32[]{:S(2)}, u32[]{:S(2)}) collective-permute-start(bf16[256,1024]{1,0:T(8,128)(2,1)S(1)} %pad_maximum_fusion.5), channel_id=1, source_target_pairs={{8,0},{0,8},{24,16},{16,24},{9,1},{1,9},{25,17},{17,25},{10,2},{2,... | collective-permute-start | bytes 1572872 | tf_op jit(solution)/shard_map/cond/branch_2_fun/ppermute | solution.py:286
  177.9 6.4 %collective-permute-start.24 = (bf16[128,1024]{1,0:T(8,128)(2,1)S(1)}, bf16[128,1024]{1,0:T(8,128)(2,1)S(1)}, u32[]{:S(2)}, u32[]{:S(2)}) collective-permute-start(bf16[128,1024]{1,0:T(8,128)(2,1)S(1)} %add_convert_fusion.7), channel_id=1, source_target_pairs={{24,8},{16,0},{8,24},{0,16},{25,9},{17,1},{9,25},{1,17},{26,10},{1... | collective-permute-start | bytes 786440 | tf_op jit(solution)/shard_map/cond/branch_2_fun/ppermute | solution.py:286
  179.4 9.2 %collective-permute-start.28 = (bf16[128,1024]{1,0:T(8,128)(2,1)S(1)}, bf16[128,1024]{1,0:T(8,128)(2,1)S(1)}, u32[]{:S(2)}, u32[]{:S(2)}) collective-permute-start(bf16[128,1024]{1,0:T(8,128)(2,1)S(1)} %add_convert_fusion.6), channel_id=1, source_target_pairs={{24,16},{16,24},{8,0},{0,8},{25,17},{17,25},{9,1},{1,9},{26,18},{1... | collective-permute-start | bytes 786440 | tf_op jit(solution)/shard_map/cond/branch_2_fun/ppermute | solution.py:286
  184.4 14.4 %slice-start.1 = ((s8[12582912]{0:T(1024)(128)(4,1)}), s8[4194304]{0:T(1024)(128)(4,1)S(1)}, s32[]{:S(2)}) async-start(s8[12582912]{0:T(1024)(128)(4,1)} %bitcast.12), calls=%async_computation.8 | async-start | bytes 8388608 | tf_op jit(solution)/shard_map/cond
  184.5 11.7 %collective-permute-start.25 = (bf16[256,1024]{1,0:T(8,128)(2,1)S(1)}, bf16[256,1024]{1,0:T(8,128)(2,1)S(1)}, u32[]{:S(2)}, u32[]{:S(2)}) collective-permute-start(bf16[256,1024]{1,0:T(8,128)(2,1)S(1)} %pad_maximum_fusion.7), channel_id=1, source_target_pairs={{24,16},{16,24},{8,0},{0,8},{25,17},{17,25},{9,1},{1,9},{26,18},{1... | collective-permute-start | bytes 1572872 | tf_op jit(solution)/shard_map/cond/branch_2_fun/ppermute | solution.py:286
  188.6 9.2 %collective-permute-start.29 = (bf16[256,1024]{1,0:T(8,128)(2,1)S(1)}, bf16[256,1024]{1,0:T(8,128)(2,1)S(1)}, u32[]{:S(2)}, u32[]{:S(2)}) collective-permute-start(bf16[256,1024]{1,0:T(8,128)(2,1)S(1)} %pad_maximum_fusion.8), channel_id=1, source_target_pairs={{24,8},{16,0},{8,24},{0,16},{25,9},{17,1},{9,25},{1,17},{26,10},{1... | collective-permute-start | bytes 1572872 | tf_op jit(solution)/shard_map/cond/branch_2_fun/ppermute | solution.py:286
  198.1 2.2 %slice-start.2 = ((s8[12582912]{0:T(1024)(128)(4,1)}), s8[4194304]{0:T(1024)(128)(4,1)S(1)}, s32[]{:S(2)}) async-start(s8[12582912]{0:T(1024)(128)(4,1)} %bitcast.12), calls=%async_computation.9 | async-start | bytes 8388608 | tf_op jit(solution)/shard_map/cond
Sparse Core Ops, SparseCore 0:
  14.1 31.7 all-gather.15
  47.6 28.5 all-gather.17
  85.9 28.1 all-gather.19

commit v2 on v1

--- a/solution.py
+++ b/solution.py
@@ -341,17 +341,21 @@
             width = d_model // 3
             early = to_slot(masked[:, 2 * width :], 1)
             hidden = hidden_transposed(gate_pre, up_pre)
-            theirs = to_slot(after(hidden, early), 1)
+            weight = weight_transposed(master)
+            high = hidden.shape[0] // 2
+            top = to_slot(after(hidden[:high], early), 1)
+            low = to_slot(hidden[high:], 1)
+            theirs = jnp.concatenate([top, low])
             one = gather(masked[:, :width])
-            two = gather(after(masked[:, width:], one))
-            last = gather(after(early, two))
+            two = gather(after(masked[:, width:], (one, top, weight)))
             half = one.shape[0] // 2
 
             def to_partner(whole):
                 return to_slot(lax.dynamic_slice(whole, (core * half, 0), (half, width)), 1)
 
-            weight = weight_transposed(master)
-            first = to_partner(after(one, weight))
+            first = to_partner(one)
+            rest = to_core(first)
+            last = gather(after(early, (two, rest)))
             second = to_partner(two)
             flags = jnp.stack([share(1).astype(jnp.int32), core * half, (1 - core) * half])
             layout = [(0, None, 0, 0, width), (1, None, 0, width, 2 * width)]
@@ -361,7 +365,7 @@
             )
             layout = [(0, None, (1,), 0, width), (1, None, (2,), 0, width)]
             ready = phase_call(
-                flags, [first, to_core(first)], layout, theirs, grad=grad, d_model=width
+                flags, [first, rest], layout, theirs, grad=grad, d_model=width
             )[0]
             second = after(second, grad)
             layout = [

time: 214 us -> 187 us (0.87)
  starting transfers between devices: 26.4 us -> 7.23 us
  waiting for transfers between devices: 94.1 us -> 83.7 us
  Pallas kernels: 52.9 us -> 60.9 us
  other arithmetic: 13.5 us -> 5.63 us
    ppermute x24 -> x7, starting transfers between devices: 26.3 us -> 6.92 us  [send(): return lax.ppermute(value, axis, pairs[::-1] if back else pairs)]
    pallas_call x4 -> x3, Pallas kernels: 34.1 us -> 48.5 us  [phase_call(): pl.pallas_call(functools.partial(phase_kernel, len(pieces), cut, wide, bl...]
    all_gather x3, waiting for transfers between devices: 31.9 us -> 19.5 us  [gather(): return lax.all_gather(block, 'shard', axis=0, tiled=True)]
    pallas_call x1 -> x0, Pallas kernels: 6.52 us -> none  [update_call(): pl.pallas_call(update_kernel, grid=(ffw // 128,), in_specs=[full] + [part...]
    convert_element_type x12 -> x0, other arithmetic: 5.41 us -> none  [all_sum(): (keep.astype(jnp.float32) + got.astype(jnp.float32)).astype(part.dtype)]
    select_n x12 -> x0, other arithmetic: 2.8 us -> none  [all_sum(): jnp.where(side == 0, part, got)]
    ppermute x24 -> x7, waiting for transfers between devices: 62.1 us -> 64.1 us  [send(): return lax.ppermute(value, axis, pairs[::-1] if back else pairs)]
    slice x4 -> x3, local copies, waits for them, and re-layouts: 6.18 us -> 4.65 us  [the longest x1 3.03 us: body(): low = to_slot(hidden[high:], 1)]
  transfers between devices with their start and end apart: 27 -> 10, of which waited for: 14 -> 6; matrix products, arithmetic and copies ran while one was open for 7% -> 7% of each run, Pallas kernels for 19% -> 23%
where the time goes in v2:
time: 187 us; the launch traced here: 186 us
  waiting for transfers between devices  83.7 us (45%)
  Pallas kernels  60.9 us (33%)
  between operations  15 us (8%)
  local copies, waits for them, and re-layouts  12.5 us (7%)
  starting transfers between devices  7.23 us (4%)
  other arithmetic  5.63 us (3%)
    ppermute x7, waiting for transfers between devices, send(): return lax.ppermute(value, axis, pairs[::-1] if back else pairs)  64.1 us
    pallas_call x3, Pallas kernels, phase_call(): pl.pallas_call(functools.partial(phase_kernel, len(pieces), cut, wide, bl...  48.5 us
    all_gather x3, waiting for transfers between devices, gather(): return lax.all_gather(block, 'shard', axis=0, tiled=True)  19.5 us
    pallas_call x1, Pallas kernels, weight_transposed(): pl.pallas_call(weight_kernel, grid=(ffw // tall,), in_specs=[pl.BlockSpec...  7.94 us
    ppermute x7, starting transfers between devices, send(): return lax.ppermute(value, axis, pairs[::-1] if back else pairs)  6.92 us
    pallas_call x1, Pallas kernels, hidden_transposed(): pl.pallas_call(hidden_kernel, grid=(rows // tall,), in_specs=[block, bloc...  4.48 us
    dynamic_slice x2, local copies, waits for them, and re-layouts, to_partner(): return to_slot(lax.dynamic_slice(whole, (core * half, 0), (half, width)), 1)  4.34 us
  transfers between devices with their start and end apart: 10, of which 6 were waited for; matrix products, arithmetic and copies ran while one was open for 7% of the time, Pallas kernels for 23%

profile of v2, /device:TPU:0, one launch (start us, length us, event | category | flops | bytes accessed | tf_op | source)
XLA Modules:
  0.0 186.4 jit_solution(7259073188901616404)
XLA Ops:
  7.2 0.8 broadcast_compare_fusion.2
  8.0 1.4 convert_reduce_fusion
  10.7 169.1 %conditional.1 = ((bf16[1,1024,1024]{2,1,0:T(8,128)(2,1)}, bf16[1,1024,1024]{2,1,0:T(8,128)(2,1)}, f32[1,1024,3072]{2,1,0:T(8,128)})) conditional(s32[]{:T(128)} %clamp.3, (s32[1,1]{1,0:T(1,128)}, bf16[1,128,3072]{2,1,0:T(8,128)(2,1)}, bf16[1,1024,1024]{2,1,0:T(8,128)(2,1)}, bf16[1,1024,1024]{2,1,0:T(8,128)(2,1)}, ...), branch_computations={%region_2.3_spmd, %region_3.5_spmd, %region_5.6_spmd} | conditional | flops 21475229696 | bytes 277612640 | solution.py:416
  10.8 0.0 copy-start.1
  10.8 0.0 all-gather.10.cloned.1.call-start
  10.8 0.8 iota_compare_fusion.1
  11.6 1.3 bitcast_select_fusion.1
  12.9 0.8 fusion.3
  13.7 0.0 all-gather.10.cloned.1.call-update
  13.7 0.0 all-gather.12.cloned.1.call-start
  13.7 3.0 %collective-permute-start = (bf16[128,1024]{1,0:T(8,128)(2,1)S(1)}, bf16[128,1024]{1,0:T(8,128)(2,1)S(1)}, u32[]{:S(2)}, u32[]{:S(2)}) collective-permute-start(bf16[128,1024]{1,0:T(8,128)(2,1)S(1)} %get-tuple-element.109), channel_id=1, source_target_pairs={{0,8},{8,0},{16,24},{24,16},{1,9},{9,1},{17,25},{25,17},{2,10},{10... | collective-permute-start | bytes 786440 | tf_op jit(solution)/shard_map/cond/branch_1_fun/ppermute | solution.py:286
  16.7 0.0 copy-done.1
  16.7 4.5 %branch_1_fun.5.refs_2_ = bf16[1024,1024]{1,0:T(8,128)(2,1)} custom-call(bf16[1,1024,1024]{2,1,0:T(8,128)(2,1)S(1)} %copy-done.1, bf16[1,1024,1024]{2,1,0:T(8,128)(2,1)} %get-tuple-element.54.up_ref.refs_5_), custom_call_target="tpu_custom_call" | custom-call | tf_op jit(solution)/shard_map/cond/branch_1_fun/pallas_call | solution.py:29
  21.2 3.0 %fusion.2 = (bf16[512,1024]{1,0:T(8,128)(2,1)}, bf16[512,1024]{1,0:T(8,128)(2,1)}) fusion(bf16[1024,1024]{1,0:T(8,128)(2,1)} %branch_1_fun.5.refs_2_), kind=kLoop, calls=%fused_computation.80 | loop fusion | bytes 4194304 | tf_op jit(solution)/shard_map/cond/branch_1_fun/slice | solution.py:347
  24.2 0.0 collective-permute-done
  24.2 0.5 collective-permute-start.1
  24.8 0.9 slice.43
  25.6 7.9 %branch_1_fun.6.refs_3_ = bf16[3072,1024]{1,0:T(8,128)(2,1)} custom-call(f32[1,1024,3072]{2,1,0:T(8,128)} %get-tuple-element.56.master_ref.refs_4_), custom_call_target="tpu_custom_call" | custom-call | bytes 18874368 | tf_op jit(solution)/shard_map/cond/branch_1_fun/pallas_call | solution.py:45
  33.6 0.0 copy-done.14
  33.6 15.6 %collective-permute-done.1 = bf16[512,1024]{1,0:T(8,128)(2,1)} collective-permute-done((bf16[512,1024]{1,0:T(8,128)(2,1)}, bf16[512,1024]{1,0:T(8,128)(2,1)}, u32[]{:S(2)}, u32[]{:S(2)}) %collective-permute-start.1) | collective-permute-done | bytes 1048608 | tf_op jit(solution)/shard_map/cond/branch_1_fun/ppermute | solution.py:286
  49.2 0.0 all-gather.12.cloned.1.call-update
  49.2 0.2 all-gather.14.cloned.1.call-start
  49.4 1.3 constant_dynamic-slice_fusion
  50.7 0.4 collective-permute-start.5
  51.1 23.4 %collective-permute-done.5.refs_0_ = bf16[512,1024]{1,0:T(8,128)(2,1)S(1)} collective-permute-done((bf16[512,1024]{1,0:T(8,128)(2,1)S(1)}, bf16[512,1024]{1,0:T(8,128)(2,1)S(1)}, u32[]{:S(2)}, u32[]{:S(2)}) %collective-permute-start.5) | collective-permute-done | bytes 1048608 | tf_op jit(solution)/shard_map/cond/branch_1_fun/ppermute | solution.py:286
  74.5 0.0 collective-permute-start.6
  74.5 2.8 %collective-permute-done.6.refs_1_ = bf16[512,1024]{1,0:T(8,128)(2,1)} collective-permute-done((bf16[512,1024]{1,0:T(8,128)(2,1)S(1)}, bf16[512,1024]{1,0:T(8,128)(2,1)}, u32[]{:S(2)}, u32[]{:S(2)}) %collective-permute-start.6) | collective-permute-done | bytes 1048608 | tf_op jit(solution)/shard_map/cond/branch_1_fun/ppermute | solution.py:286
  77.3 19.5 %all-gather.12.cloned.1.call-done.refs_1_ = bf16[1024,2048]{1,0:T(8,128)(2,1)} async-done(((bf16[128,2048]{1,0:T(8,128)(2,1)}), bf16[1024,2048]{1,0:T(8,128)(2,1)}) %all-gather.12.cloned.1.call-update) | async-done | bytes 4194320 | tf_op jit(solution)/shard_map/cond/branch_1_fun/all_gather | solution.py:337
  96.8 0.0 all-gather.14.cloned.1.call-update
  96.9 1.5 collective-permute-start.2
  98.4 0.7 and_reduce_fusion
  99.7 0.6 pad_add_fusion.flag_ref
  100.4 1.3 constant_dynamic-update-slice_fusion.1
  101.7 0.0 copy-start.5
  101.7 20.9 %collective-permute-done.2 = bf16[512,1024]{1,0:T(8,128)(2,1)} collective-permute-done((bf16[512,1024]{1,0:T(8,128)(2,1)}, bf16[512,1024]{1,0:T(8,128)(2,1)}, u32[]{:S(2)}, u32[]{:S(2)}) %collective-permute-start.2) | collective-permute-done | bytes 1048608 | tf_op jit(solution)/shard_map/cond/branch_1_fun/ppermute | solution.py:286
  122.5 1.3 constant_dynamic-update-slice_fusion.refs_2_.refs_3_
  123.8 0.0 copy-done.10
  123.8 0.0 copy-start.7
  123.9 3.0 %constant_dynamic-slice_fusion.1 = bf16[512,1024]{1,0:T(8,128)(2,1)} fusion(bf16[1024,2048]{1,0:T(8,128)(2,1)} %all-gather.12.cloned.1.call-done.refs_1_, s32[]{:T(128)S(6)} %select_n.151), kind=kLoop, calls=%fused_computation.8 | loop fusion | bytes 2097156 | tf_op jit(solution)/shard_map/cond/branch_1_fun/dynamic_slice | solution.py:354
  126.9 1.5 collective-permute-start.3
  128.4 21.8 %branch_1_fun.7 = (bf16[1,1024,1024]{2,1,0:T(8,128)(2,1)}, bf16[1,1024,1024]{2,1,0:T(8,128)(2,1)}, bf16[1024,3072]{1,0:T(8,128)(2,1)}) custom-call(s32[3]{0:T(128)} %pad_add_fusion.flag_ref, bf16[1024,1024]{1,0:T(8,128)(2,1)} %all-gather.10.cloned.1.call-done.refs_0_, bf16[1024,2048]{1,0:T(8,128)(2,1)} %all-gather.12.cloned.1.call-done.refs_1_, ...), custom_call_target="tpu_custom_call" | custom-call | flops 12884901888 | bytes 25165824 | tf_op jit(solution)/shard_map/cond/branch_1_fun/pallas_call | solution.py:219
  150.2 1.4 collective-permute-done.3.refs_0_
  151.6 0.0 collective-permute-start.4
  151.6 8.2 %branch_1_fun.8.refs_6_ = bf16[1024,1024]{1,0:T(8,128)(2,1)} custom-call(s32[3]{0:T(128)} %pad_add_fusion.flag_ref, bf16[512,1024]{1,0:T(8,128)(2,1)} %copy-done.10, bf16[512,1024]{1,0:T(8,128)(2,1)} %collective-permute-done.6.refs_1_, bf16[1024,1024]{1,0:T(8,128)(2,1)} %copy-done.7, bf16[1024,3072]{1,0:T(8,128)(2,1)} %get-tuple-element.62.refs_3_.refs_5_), custom_call_target="tpu_custom_call" | custom-call | flops 2147483648 | bytes 8388608 | tf_op jit(solution)/shard_map/cond/branch_1_fun/pallas_call | solution.py:219
  159.8 0.0 collective-permute-done.4.refs_1_
  159.8 0.0 all-gather.14.cloned.1.call-done.refs_2_
  159.8 0.9 copy-done.13
  160.8 18.5 %branch_1_fun.9 = f32[1,1024,3072]{2,1,0:T(8,128)} custom-call(s32[3]{0:T(128)} %pad_add_fusion.flag_ref, bf16[512,1024]{1,0:T(8,128)(2,1)} %copy-done.12, bf16[512,1024]{1,0:T(8,128)(2,1)} %copy-done.13, bf16[1024,1024]{1,0:T(8,128)(2,1)} %all-gather.14.cloned.1.call-done.refs_2_, bf16[1024,1024]{1,0:T(8,128)(2,1)} %copy-done.7, ...), custom_call_target="tpu_custom_call" | custom-call | flops 6442450944 | bytes 25165824 | tf_op jit(solution)/shard_map/cond/branch_1_fun/pallas_call | solution.py:219
  (11 shorter events, 0.0 us)
Async XLA Ops:
  10.8 6.0 %copy-start.1 = (bf16[1,1024,1024]{2,1,0:T(8,128)(2,1)S(1)}, bf16[1,1024,1024]{2,1,0:T(8,128)(2,1)}, u32[]{:S(2)}) copy-start(bf16[1,1024,1024]{2,1,0:T(8,128)(2,1)} %get-tuple-element.53.gate_ref.refs_4_) | copy-start | bytes 6291460 | tf_op jit(solution)/shard_map/cond
  10.8 38.4 %all-gather.10.cloned.1.call-start = ((), (), s32[]{:S(2)}) async-start(), calls=%async_computation.1 | async-start | bytes 2359296 | tf_op jit(solution)/shard_map/cond/branch_1_fun/all_gather | solution.py:337
  13.7 83.2 %all-gather.12.cloned.1.call-start = ((), (), s32[]{:S(2)}) async-start(), calls=%async_computation.2 | async-start | bytes 4718592 | tf_op jit(solution)/shard_map/cond/branch_1_fun/all_gather | solution.py:337
  13.7 10.5 %collective-permute-start = (bf16[128,1024]{1,0:T(8,128)(2,1)S(1)}, bf16[128,1024]{1,0:T(8,128)(2,1)S(1)}, u32[]{:S(2)}, u32[]{:S(2)}) collective-permute-start(bf16[128,1024]{1,0:T(8,128)(2,1)S(1)} %get-tuple-element.109), channel_id=1, source_target_pairs={{0,8},{8,0},{16,24},{24,16},{1,9},{9,1},{17,25},{25,17},{2,10},{10... | collective-permute-start | bytes 786440 | tf_op jit(solution)/shard_map/cond/branch_1_fun/ppermute | solution.py:286
  24.2 9.3 %copy-start.14 = (bf16[128,1024]{1,0:T(8,128)(2,1)}, bf16[128,1024]{1,0:T(8,128)(2,1)S(1)}, u32[]{:S(2)}) copy-start(bf16[128,1024]{1,0:T(8,128)(2,1)S(1)} %collective-permute-done) | copy-start | bytes 786436 | tf_op jit(solution)/shard_map/cond
  24.2 24.9 %collective-permute-start.1 = (bf16[512,1024]{1,0:T(8,128)(2,1)}, bf16[512,1024]{1,0:T(8,128)(2,1)}, u32[]{:S(2)}, u32[]{:S(2)}) collective-permute-start(bf16[512,1024]{1,0:T(8,128)(2,1)} %get-tuple-element.55), channel_id=1, source_target_pairs={{24,16},{16,24},{8,0},{0,8},{25,17},{17,25},{9,1},{1,9},{26,18},{1... | collective-permute-start | bytes 3145736 | tf_op jit(solution)/shard_map/cond/branch_1_fun/ppermute | solution.py:286
  49.2 110.6 %all-gather.14.cloned.1.call-start = ((), (), s32[]{:S(2)}) async-start(), calls=%async_computation.3 | async-start | bytes 2359296 | tf_op jit(solution)/shard_map/cond/branch_1_fun/all_gather | solution.py:337
  50.7 23.8 %collective-permute-start.5 = (bf16[512,1024]{1,0:T(8,128)(2,1)S(1)}, bf16[512,1024]{1,0:T(8,128)(2,1)S(1)}, u32[]{:S(2)}, u32[]{:S(2)}) collective-permute-start(bf16[512,1024]{1,0:T(8,128)(2,1)S(1)} %constant_dynamic-slice_fusion), channel_id=1, source_target_pairs={{0,8},{24,16},{16,24},{8,0},{1,9},{25,17},{17,25},{9,1},{2,10},{26... | collective-permute-start | bytes 3145736 | tf_op jit(solution)/shard_map/cond/branch_1_fun/ppermute | solution.py:286
  74.5 49.3 %copy-start.10 = (bf16[512,1024]{1,0:T(8,128)(2,1)}, bf16[512,1024]{1,0:T(8,128)(2,1)S(1)}, u32[]{:S(2)}) copy-start(bf16[512,1024]{1,0:T(8,128)(2,1)S(1)} %collective-permute-done.5.refs_0_) | copy-start | bytes 3145732 | tf_op jit(solution)/shard_map/cond
  74.5 2.8 %collective-permute-start.6 = (bf16[512,1024]{1,0:T(8,128)(2,1)S(1)}, bf16[512,1024]{1,0:T(8,128)(2,1)}, u32[]{:S(2)}, u32[]{:S(2)}) collective-permute-start(bf16[512,1024]{1,0:T(8,128)(2,1)S(1)} %collective-permute-done.5.refs_0_), channel_id=1, source_target_pairs={{0,1},{1,0},{2,3},{3,2},{4,5},{5,4},{6,7},{7,6},{8,9},{9,8},{10,11... | collective-permute-start | bytes 3145736 | tf_op jit(solution)/shard_map/cond/branch_1_fun/ppermute | solution.py:286
  96.9 25.7 %collective-permute-start.2 = (bf16[512,1024]{1,0:T(8,128)(2,1)}, bf16[512,1024]{1,0:T(8,128)(2,1)}, u32[]{:S(2)}, u32[]{:S(2)}) collective-permute-start(bf16[512,1024]{1,0:T(8,128)(2,1)} %get-tuple-element.107), channel_id=1, source_target_pairs={{8,0},{16,24},{24,16},{0,8},{9,1},{17,25},{25,17},{1,9},{10,2},{18... | collective-permute-start | bytes 3145736 | tf_op jit(solution)/shard_map/cond/branch_1_fun/ppermute | solution.py:286
  101.7 26.7 %copy-start.5 = (bf16[1,1024,1024]{2,1,0:T(8,128)(2,1)S(1)}, bf16[1,1024,1024]{2,1,0:T(8,128)(2,1)}, u32[]{:S(2)}) copy-start(bf16[1,1024,1024]{2,1,0:T(8,128)(2,1)} %get-tuple-element.54.up_ref.refs_5_) | copy-start | bytes 6291460 | tf_op jit(solution)/shard_map/cond
  123.8 26.3 %copy-start.7 = (bf16[1024,1024]{1,0:T(8,128)(2,1)}, bf16[1024,1024]{1,0:T(8,128)(2,1)S(1)}, u32[]{:S(2)}) copy-start(bf16[1024,1024]{1,0:T(8,128)(2,1)S(1)} %constant_dynamic-update-slice_fusion.refs_2_.refs_3_) | copy-start | bytes 6291460 | tf_op jit(solution)/shard_map/cond
  126.9 24.7 %collective-permute-start.3 = (bf16[512,1024]{1,0:T(8,128)(2,1)}, bf16[512,1024]{1,0:T(8,128)(2,1)S(1)}, u32[]{:S(2)}, u32[]{:S(2)}) collective-permute-start(bf16[512,1024]{1,0:T(8,128)(2,1)} %constant_dynamic-slice_fusion.1), channel_id=1, source_target_pairs={{16,24},{24,16},{0,8},{8,0},{17,25},{25,17},{1,9},{9,1},{18,26},{2... | collective-permute-start | bytes 3145736 | tf_op jit(solution)/shard_map/cond/branch_1_fun/ppermute | solution.py:286
  151.6 8.2 %copy-start.12 = (bf16[512,1024]{1,0:T(8,128)(2,1)}, bf16[512,1024]{1,0:T(8,128)(2,1)S(1)}, u32[]{:S(2)}) copy-start(bf16[512,1024]{1,0:T(8,128)(2,1)S(1)} %collective-permute-done.3.refs_0_) | copy-start | bytes 3145732 | tf_op jit(solution)/shard_map/cond
  151.6 8.2 %collective-permute-start.4 = (bf16[512,1024]{1,0:T(8,128)(2,1)S(1)}, bf16[512,1024]{1,0:T(8,128)(2,1)S(1)}, u32[]{:S(2)}, u32[]{:S(2)}) collective-permute-start(bf16[512,1024]{1,0:T(8,128)(2,1)S(1)} %collective-permute-done.3.refs_0_), channel_id=1, source_target_pairs={{7,6},{6,7},{5,4},{4,5},{3,2},{2,3},{1,0},{0,1},{15,14},{14,15},{1... | collective-permute-start | bytes 3145736 | tf_op jit(solution)/shard_map/cond/branch_1_fun/ppermute | solution.py:286
  159.8 1.0 copy-start.13
Sparse Core Ops, SparseCore 0:
  13.8 31.7 all-gather.9
  49.3 47.4 all-gather.11
  98.4 27.8 all-gather.13
